TPU v7x, 256 devices: a whole 4x4x8 slice. The times are simulated.
256 devices in a mesh: expert: 64 (over x, z, core), mp: 4 (over y).
Axes of the slice: x: 4, y: 4, z: 8, core: 2. Of those that a mesh axis runs over, the one named last changes fastest.
Arguments:
- routes: int32 [8192, 8], P('expert'), may hold values from 0 to 127, all different within a row; in each aligned block of 128 rows (0 to 127, 128 to 255, ...) at most 12 rows name the same one
- routed_hidden: bfloat16 [8192, 8, 1024], P('expert', None, 'mp'), may hold values from -36 to 36
- down_proj: bfloat16 [128, 1024, 3584], P('expert', None, 'mp'), may hold values from -6 to 6
- merge_group: int32 [128], replicated, may hold values from 0 to 63, as said below
Outputs:
- merged: bfloat16 [64, 1024, 3584], P('expert', None, 'mp')
Inputs may be any that keep to these rules, and one draw needn't show every extreme that they name: `routes`: among the 128 tokens of one index of the expert axis (aligned blocks of rows) no expert is named more than 12 times, a bound that some block reaches. `merge_group`: every group holds 1 to 3 experts, and some group holds exactly 3.
All inputs are finite; a program needn't handle non-finite values.
Results may differ from a plain program's by a relative error of at most 0.0056.
Values may be sent and summed in bfloat16 or wider, within the bound.
No kernel may reach another device: no remote copies, remote signals or barrier semaphores. Data moves between devices by JAX's collectives and lax.ppermute only.
A program may use at most 128 MiB of HBM per device.

v0:
```python
import jax
import jax.numpy as jnp
from jax import lax
from jax.sharding import PartitionSpec as P

GMAX = 3


damping = 0.1
epsilon = 1e-05


def slot_rank(labels, label_count):
    onehot = (labels[:, None] == jnp.arange(label_count, dtype=jnp.int32)[None, :]).astype(
        jnp.int32
    )
    return jnp.sum(onehot * (jnp.cumsum(onehot, axis=0) - 1), axis=1)


def member_table(merge_group, group_count):
    expert_total = merge_group.shape[0]
    position = slot_rank(merge_group, group_count)
    slot_table = jnp.full((group_count * GMAX,), -1, jnp.int32)
    slot_table = slot_table.at[merge_group * GMAX + position].set(
        jnp.arange(expert_total, dtype=jnp.int32)
    )
    return slot_table.reshape(group_count, GMAX).T


def select_members(pieces, members):
    local_count = pieces.shape[0]
    present = members >= 0
    chosen = jnp.maximum(members, 0)
    picked = pieces[chosen % local_count, chosen // local_count]
    return jnp.where(present[:, :, None, None], picked, jnp.zeros((), pieces.dtype))


def solve_group(gram_sum, partial_value):
    order_size = gram_sum.shape[0]
    ridge_term = damping * jnp.trace(gram_sum) / order_size + epsilon
    system = gram_sum + ridge_term * jnp.eye(order_size, dtype=jnp.float32)
    factor = jnp.linalg.cholesky(system)
    return jax.scipy.linalg.cho_solve((factor, True), partial_value)


def member_work(member_rows, member_weights):
    gram_sum = jnp.einsum(
        "rsf,rsg->fg", member_rows, member_rows, preferred_element_type=jnp.float32
    )
    projected = jnp.einsum(
        "rsf,rfd->rsd", member_rows, member_weights, preferred_element_type=jnp.float32
    ).astype(jnp.bfloat16)
    partial_value = jnp.einsum(
        "rsf,rsd->fd", member_rows, projected, preferred_element_type=jnp.float32
    )
    return (gram_sum, partial_value)


def on_device(routes, routed_hidden, down_proj, merge_group):
    expert_count = lax.axis_size("expert")
    local_count = down_proj.shape[0]
    expert_total = local_count * expert_count
    tok_count, top_count = routes.shape
    hidden_part = routed_hidden.shape[2]
    full_width = down_proj.shape[1]
    out_part = down_proj.shape[2]
    slot_cap = 3 * tok_count * top_count // (2 * expert_total)
    row_count = tok_count * top_count
    targets = routes.reshape(row_count)
    position = slot_rank(targets, expert_total)
    members = member_table(merge_group, expert_count)
    piece_rows = full_width // expert_count
    member_rank = slot_rank(merge_group, expert_count)
    layer_index = member_rank[targets]
    dest_device = merge_group[targets]
    layer_count = GMAX
    slot_index = (layer_index * expert_count + dest_device) * slot_cap + position
    source_row = jnp.full((layer_count * expert_count * slot_cap,), row_count, jnp.int32)
    source_row = source_row.at[slot_index].set(jnp.arange(row_count, dtype=jnp.int32))
    padded = jnp.concatenate(
        [
            routed_hidden.reshape(row_count, hidden_part),
            jnp.zeros((1, hidden_part), routed_hidden.dtype),
        ],
        axis=0,
    )
    outgoing = padded[source_row].reshape(layer_count, expert_count * slot_cap, hidden_part)
    arrived = lax.all_to_all(outgoing, "expert", split_axis=1, concat_axis=1, tiled=True)
    expert_rows = lax.all_gather(arrived, "mp", axis=2, tiled=True)
    weight_pieces = down_proj.reshape(local_count, expert_count, piece_rows, out_part)
    weights_all = lax.all_to_all(weight_pieces, "expert", split_axis=1, concat_axis=1, tiled=True)
    weights_mine = lax.all_to_all(
        select_members(weights_all, members), "expert", split_axis=1, concat_axis=1, tiled=True
    )
    member_weights = weights_mine.reshape(GMAX, full_width, out_part)
    gram_sum, partial_value = member_work(expert_rows, member_weights)
    merged = solve_group(gram_sum, partial_value)
    return merged.astype(jnp.bfloat16).reshape(1, full_width, out_part)


def solution(mesh):
    return jax.shard_map(
        on_device,
        mesh=mesh,
        in_specs=(P("expert", None), P("expert", None, "mp"), P("expert", None, "mp"), P()),
        out_specs=P("expert", None, "mp"),
        check_vma=False,
    )
```

profile of v0, /device:TPU:1, one launch (start us, length us, event | category | flops | bytes accessed | tf_op | source)
XLA Modules:
  0.0 604.8 jit_solution(14957902359115608196)
XLA Ops:
  8.4 6.6 %gather_fusion.1 = s32[1024]{0:T(1024)S(1)} fusion(s32[128]{0:T(128)S(1)} %copy-done, s32[1024]{0:T(1024)S(1)} %broadcast_clamp_fusion), kind=kCustom, calls=%fused_computation.1 | custom fusion | bytes 12288 | tf_op jit(solution)/shard_map/gather | solution.py:75
  15.4 6.6 %gather_fusion = s32[1024]{0:T(1024)S(1)} fusion(s32[128]{0:T(128)S(1)} %select_reduce_fusion.9, s32[1024]{0:T(1024)S(1)} %broadcast_clamp_fusion), kind=kCustom, calls=%fused_computation | custom fusion | bytes 12288 | tf_op jit(solution)/shard_map/gather | solution.py:74
  27.2 6.9 %gather_fusion.2 = bf16[2304,256]{1,0:T(8,128)(2,1)S(1)} fusion(bf16[1025,256]{1,0:T(8,128)(2,1)S(1)} %concatenate.68, s32[3072]{0:T(1024)S(1)} %pad_clamp_fusion), kind=kCustom, calls=%fused_computation.2 | custom fusion | bytes 2368512 | tf_op jit(solution)/shard_map/gather | solution.py:87
  36.3 13.0 %all-to-all-start = ((bf16[3,768,256]{2,0,1:T(4,128)(2,1)}), bf16[3,768,256]{2,0,1:T(4,128)(2,1)S(1)}, u32[]{:S(2)}, u32[]{:S(2)}) async-start(bf16[3,768,256]{2,0,1:T(4,128)(2,1)} %copy.45), calls=%async_computation | async-start | bytes 3145728 | tf_op jit(solution)/shard_map/all_to_all | solution.py:88
  53.4 35.6 %all-to-all-done = bf16[3,768,256]{2,0,1:T(4,128)(2,1)S(1)} async-done(((bf16[3,768,256]{2,0,1:T(4,128)(2,1)}), bf16[3,768,256]{2,0,1:T(4,128)(2,1)S(1)}, u32[]{:S(2)}, u32[]{:S(2)}) %all-to-all-start) | async-done | bytes 1179680 | tf_op jit(solution)/shard_map/all_to_all | solution.py:88
  89.1 6.3 %all-to-all-start.1 = ((bf16[2,64,16,896]{3,2,0,1:T(8,128)(2,1)}), bf16[2,64,16,896]{3,2,0,1:T(8,128)(2,1)}, u32[]{:S(2)}, u32[]{:S(2)}) async-start(bf16[2,64,16,896]{3,2,0,1:T(8,128)(2,1)} %copy.49), calls=%async_computation.1 | async-start | bytes 7340032 | tf_op jit(solution)/shard_map/all_to_all | solution.py:91
  98.4 81.6 %all-to-all-done.1 = bf16[2,64,16,896]{3,2,0,1:T(8,128)(2,1)} async-done(((bf16[2,64,16,896]{3,2,0,1:T(8,128)(2,1)}), bf16[2,64,16,896]{3,2,0,1:T(8,128)(2,1)}, u32[]{:S(2)}, u32[]{:S(2)}) %all-to-all-start.1) | async-done | bytes 3670048 | tf_op jit(solution)/shard_map/all_to_all | solution.py:91
  180.0 6.6 %gather_fusion.3 = bf16[192,16,896]{2,1,0:T(8,128)(2,1)} fusion(bf16[2,64,16,896]{3,2,0,1:T(8,128)(2,1)} %all-to-all-done.1, s32[192]{0:T(256)S(1)} %reshape.383), kind=kCustom, calls=%fused_computation.3 | custom fusion | bytes 11011584 | tf_op jit(solution)/shard_map/gather | solution.py:34
  186.6 6.2 %copy_select_fusion = bf16[3,64,16,896]{3,2,0,1:T(8,128)(2,1)} fusion(bf16[3,64,16,896]{3,2,1,0:T(8,128)(2,1)} %bitcast.191, pred[3,64]{0,1:T(8,128)(4,1)S(1)} %bitcast.196), kind=kLoop, calls=%fused_computation.8 | loop fusion | flops 2752512 | bytes 11010240 | tf_op jit(solution)/shard_map/jit(_where)/select_n | solution.py:35
  192.8 6.3 %all-to-all-start.2 = ((bf16[3,64,16,896]{3,2,0,1:T(8,128)(2,1)}), bf16[3,64,16,896]{3,2,0,1:T(8,128)(2,1)}, u32[]{:S(2)}, u32[]{:S(2)}) async-start(bf16[3,64,16,896]{3,2,0,1:T(8,128)(2,1)} %copy_select_fusion), calls=%async_computation.2 | async-start | bytes 11010048 | tf_op jit(solution)/shard_map/all_to_all | solution.py:92
  199.2 10.7 %select_reduce_fusion = (f32[]{:T(128)}, f32[1024,1024]{1,0:T(8,128)}) fusion(bf16[3,768,1024]{2,1,0:T(8,128)(2,1)} %all-gather.2.cloned.1.call-done), kind=kOutput, calls=%fused_computation.14 | convolution fusion | flops 4834983936 | bytes 8912900 | tf_op jit(solution)/shard_map/rsf,rsg->fg/dot_general | solution.py:47
  209.9 5.4 copy.48
  222.3 11.7 %cholesky.223 = f32[128,128]{1,0:T(8,128)S(1)} custom-call(f32[128,128]{1,0:T(8,128)S(1)} %cholesky.580), custom_call_target="Cholesky" | custom-call | tf_op jit(solution)/shard_map/jit(cholesky)/cholesky | solution.py:42
  234.1 9.8 %custom-call.66 = f32[1,128,128]{1,2,0:T(8,128)S(1)} custom-call(f32[1,128,128]{2,1,0:T(8,128)S(1)} %get-tuple-element.61), custom_call_target="InvertDiagBlocksLowerTriangular" | custom-call | tf_op jit(solution)/shard_map/jit(cholesky)/cholesky | solution.py:42
  250.3 20.4 %cholesky.244 = f32[128,128]{1,0:T(8,128)S(1)} custom-call(f32[128,128]{1,0:T(8,128)S(1)} %cholesky.584), custom_call_target="Cholesky" | custom-call | tf_op jit(solution)/shard_map/jit(cholesky)/cholesky | solution.py:42
  271.3 9.8 %custom-call.67 = f32[1,128,128]{1,2,0:T(8,128)S(1)} custom-call(f32[1,128,128]{2,1,0:T(8,128)S(1)} %get-tuple-element.58), custom_call_target="InvertDiagBlocksLowerTriangular" | custom-call | tf_op jit(solution)/shard_map/jit(cholesky)/cholesky | solution.py:42
  284.5 11.7 %cholesky.468 = f32[128,128]{1,0:T(8,128)S(1)} custom-call(f32[128,128]{1,0:T(8,128)S(1)} %cholesky.589), custom_call_target="Cholesky" | custom-call | tf_op jit(solution)/shard_map/jit(cholesky)/cholesky | solution.py:42
  296.9 9.8 %custom-call.68 = f32[1,128,128]{1,2,0:T(8,128)S(1)} custom-call(f32[1,128,128]{2,1,0:T(8,128)S(1)} %get-tuple-element.55), custom_call_target="InvertDiagBlocksLowerTriangular" | custom-call | tf_op jit(solution)/shard_map/jit(cholesky)/cholesky | solution.py:42
  310.3 11.9 %cholesky.487 = f32[128,128]{1,0:T(8,128)S(1)} custom-call(f32[128,128]{1,0:T(8,128)S(1)} %cholesky.594), custom_call_target="Cholesky" | custom-call | tf_op jit(solution)/shard_map/jit(cholesky)/cholesky | solution.py:42
  322.8 9.8 %custom-call.69 = f32[1,128,128]{1,2,0:T(8,128)S(1)} custom-call(f32[1,128,128]{2,1,0:T(8,128)S(1)} %get-tuple-element.52), custom_call_target="InvertDiagBlocksLowerTriangular" | custom-call | tf_op jit(solution)/shard_map/jit(cholesky)/cholesky | solution.py:42
  336.1 11.7 %cholesky.506 = f32[128,128]{1,0:T(8,128)S(1)} custom-call(f32[128,128]{1,0:T(8,128)S(1)} %cholesky.599), custom_call_target="Cholesky" | custom-call | tf_op jit(solution)/shard_map/jit(cholesky)/cholesky | solution.py:42
  348.4 10.2 %custom-call.70 = f32[1,128,128]{1,2,0:T(8,128)S(1)} custom-call(f32[1,128,128]{2,1,0:T(8,128)S(1)} %get-tuple-element.49), custom_call_target="InvertDiagBlocksLowerTriangular" | custom-call | tf_op jit(solution)/shard_map/jit(cholesky)/cholesky | solution.py:42
  362.0 11.7 %cholesky.526 = f32[128,128]{1,0:T(8,128)S(1)} custom-call(f32[128,128]{1,0:T(8,128)S(1)} %cholesky.604), custom_call_target="Cholesky" | custom-call | tf_op jit(solution)/shard_map/jit(cholesky)/cholesky | solution.py:42
  374.3 9.8 %custom-call.71 = f32[1,128,128]{1,2,0:T(8,128)S(1)} custom-call(f32[1,128,128]{2,1,0:T(8,128)S(1)} %get-tuple-element.46), custom_call_target="InvertDiagBlocksLowerTriangular" | custom-call | tf_op jit(solution)/shard_map/jit(cholesky)/cholesky | solution.py:42
  387.1 11.7 %cholesky.546 = f32[128,128]{1,0:T(8,128)S(1)} custom-call(f32[128,128]{1,0:T(8,128)S(1)} %cholesky.609), custom_call_target="Cholesky" | custom-call | tf_op jit(solution)/shard_map/jit(cholesky)/cholesky | solution.py:42
  399.5 9.9 %custom-call.72 = f32[1,128,128]{1,2,0:T(8,128)S(1)} custom-call(f32[1,128,128]{2,1,0:T(8,128)S(1)} %get-tuple-element.43), custom_call_target="InvertDiagBlocksLowerTriangular" | custom-call | tf_op jit(solution)/shard_map/jit(cholesky)/cholesky | solution.py:42
  412.1 11.7 %cholesky.564 = f32[128,128]{1,0:T(8,128)S(1)} custom-call(f32[128,128]{1,0:T(8,128)S(1)} %convolution_subtract_fusion.16), custom_call_target="Cholesky" | custom-call | tf_op jit(solution)/shard_map/jit(cholesky)/cholesky | solution.py:42
  434.1 4.8 select_select_fusion
  438.9 23.0 %while.1 = (s32[]{:T(128)}, f32[1024,1024]{1,0:T(8,128)}, s32[8,2]{0,1:T(2,128)S(1)}, f32[8,128,128]{2,1,0:T(8,128)S(1)}, s32[]{:T(128)}) while((s32[]{:T(128)}, f32[1024,1024]{1,0:T(8,128)}, s32[8,2]{0,1:T(2,128)S(1)}, f32[8,128,128]{2,1,0:T(8,128)S(1)}, s32[]{:T(128)}) %tuple.60), condition=%wide.while_cond, body=%wide.while_body.sunk | while | flops 2 | bytes 131189 | solution.py:43
  461.9 78.8 %custom-call.73 = f32[8,128,128]{1,2,0:T(8,128)S(1)} custom-call(f32[8,128,128]{2,1,0:T(8,128)S(1)} %get-tuple-element.12), custom_call_target="InvertDiagBlocksLowerTriangular" | custom-call | tf_op jit(solution)/shard_map/jit(_cho_solve)/triangular_solve | solution.py:43
  540.8 5.5 copy.52
  546.2 17.1 %fusion.4 = f32[1024,896]{1,0:T(8,128)} fusion(bf16[3,768,1024]{2,1,0:T(8,128)(2,1)} %all-gather.2.cloned.1.call-done, bf16[3,1024,896]{2,1,0:T(8,128)(2,1)} %bitcast.192), kind=kOutput, calls=%fused_computation.20 | convolution fusion | flops 8457781248 | bytes 13893632 | tf_op jit(solution)/shard_map/rsf,rsd->fd/dot_general | solution.py:53
  (172 shorter events, 114.8 us)
Async XLA Ops:
  6.5 1.9 copy-start
  15.4 11.8 %copy-start.4 = (bf16[128,8,256]{2,1,0:T(8,128)(2,1)S(1)}, bf16[128,8,256]{2,1,0:T(8,128)(2,1)}, u32[]{:S(2)}) copy-start(bf16[128,8,256]{2,1,0:T(8,128)(2,1)} %param.5) | copy-start | bytes 1572868
  36.3 52.8 %all-to-all-start = ((bf16[3,768,256]{2,0,1:T(4,128)(2,1)}), bf16[3,768,256]{2,0,1:T(4,128)(2,1)S(1)}, u32[]{:S(2)}, u32[]{:S(2)}) async-start(bf16[3,768,256]{2,0,1:T(4,128)(2,1)} %copy.45), calls=%async_computation | async-start | bytes 3145728 | tf_op jit(solution)/shard_map/all_to_all | solution.py:88
  89.1 91.0 %all-to-all-start.1 = ((bf16[2,64,16,896]{3,2,0,1:T(8,128)(2,1)}), bf16[2,64,16,896]{3,2,0,1:T(8,128)(2,1)}, u32[]{:S(2)}, u32[]{:S(2)}) async-start(bf16[2,64,16,896]{3,2,0,1:T(8,128)(2,1)} %copy.49), calls=%async_computation.1 | async-start | bytes 7340032 | tf_op jit(solution)/shard_map/all_to_all | solution.py:91
  95.4 103.8 %all-gather.2.cloned.1.call-start = ((), (), s32[]{:S(2)}) async-start(), calls=%async_computation.3 | async-start | bytes 5898240 | tf_op jit(solution)/shard_map/all_gather | solution.py:89
  192.8 347.9 %all-to-all-start.2 = ((bf16[3,64,16,896]{3,2,0,1:T(8,128)(2,1)}), bf16[3,64,16,896]{3,2,0,1:T(8,128)(2,1)}, u32[]{:S(2)}, u32[]{:S(2)}) async-start(bf16[3,64,16,896]{3,2,0,1:T(8,128)(2,1)} %copy_select_fusion), calls=%async_computation.2 | async-start | bytes 11010048 | tf_op jit(solution)/shard_map/all_to_all | solution.py:92
  220.3 2.0 copy-start.2
  563.3 4.0 copy-start.1
  566.7 3.3 copy-start.3
  595.8 1.2 copy-start.5
Sparse Core Ops, SparseCore 0:
  98.0 59.2 all-gather.1
where the time goes:
time: 615 us; the launch traced here: 605 us
  other arithmetic  278 us (45%)
  waiting for transfers between devices  117 us (19%)
  matrix products  82.2 us (13%)
  local copies, waits for them, and re-layouts  81.4 us (13%)
  starting transfers between devices  25.6 us (4%)
  between operations  20.3 us (3%)
    another operation x30, other arithmetic, solve_group(): factor = jnp.linalg.cholesky(system)  181 us
    another operation x4, other arithmetic, solve_group(): return jax.scipy.linalg.cho_solve((factor, True), partial_value)  84.4 us
    all_to_all x1, waiting for transfers between devices, on_device(): lax.all_to_all(weight_pieces, 'expert', split_axis=1, concat_axis=1, tile...  81.6 us
    all_to_all x1, waiting for transfers between devices, on_device(): lax.all_to_all(outgoing, 'expert', split_axis=1, concat_axis=1, tiled=True)  35.6 us
    another operation x30, matrix products, solve_group(): return jax.scipy.linalg.cho_solve((factor, True), partial_value)  31.3 us
    another operation x14, matrix products, solve_group(): factor = jnp.linalg.cholesky(system)  23.1 us
    another operation x26, local copies, waits for them, and re-layouts  22.9 us
    dot_general x1, matrix products, member_work(): jnp.einsum('rsf,rsd->fd', member_rows, projected, preferred_element_type=...  17.1 us
  transfers between devices with their start and end apart: 4, of which 2 were waited for; matrix products, arithmetic and copies ran while one was open for 58% of the time, Pallas kernels for 0%

commit v1 on v0

v1 whole, which is shorter than its diff:
```python
import jax
import jax.numpy as jnp
from jax import lax
from jax.experimental import pallas as pl
from jax.experimental.pallas import tpu as pltpu
from jax.sharding import PartitionSpec as P

GMAX = 3
BLK = 256
damping = 0.1
epsilon = 1e-05
F32 = jnp.float32
BF16 = jnp.bfloat16


def sweep_counts():
    gaps, delta = [], 1e-3
    for _ in range(16):
        gaps.append(1.0 - delta)
        if 2.0 * delta / (1.0 + delta) > 2.0 - 2.0 / GAIN_MAX:
            delta = (1.0 - (1.0 - delta) / GAIN_MAX) ** 0.5
        else:
            delta = (2.0 * delta / (1.0 + delta)) ** 0.5
    return gaps


GAIN_MAX = 1.85
NEWTON_GAPS = sweep_counts()


def halves(value):
    high = value.astype(BF16)
    return high, (value - high.astype(F32)).astype(BF16)


def dot(a, b):
    return jnp.dot(a, b, preferred_element_type=F32)


def dot3(a, b):
    (ah, al), (bh, bl) = a, b
    return dot(ah, bh) + (dot(ah, bl) + dot(al, bh))


def thirds(value):
    high = value.astype(BF16)
    rest = value - high.astype(F32)
    mid = rest.astype(BF16)
    return high, mid, (rest - mid.astype(F32)).astype(BF16)


def dot6(a, b):
    (ah, am, al), (bh, bm, bl) = a, b
    small = dot(am, bm) + (dot(ah, bl) + dot(al, bh))
    return dot(ah, bh) + (dot(ah, bm) + dot(am, bh) + small)


def block_inverse(block, lower):
    size = block.shape[0]
    upper = jnp.max(jnp.sum(jnp.abs(block), axis=1, keepdims=True))
    gap = 2.0 * lower / (lower + upper)
    steps = jnp.int32(0)
    for edge in NEWTON_GAPS:
        steps = steps + (gap < edge).astype(jnp.int32)
    rows = lax.broadcasted_iota(jnp.int32, (size, size), 0)
    cols = lax.broadcasted_iota(jnp.int32, (size, size), 1)
    total = jnp.full((1, size), lower + upper, F32)
    start = jnp.where(rows == cols, 2.0 / total, 0.0)
    block_parts = thirds(block)

    def step(_, carry):
        guess, delta = carry
        parts = halves(guess)
        image = dot3(block_parts[:2], parts)
        gain = jnp.minimum(2.0 / (2.0 - delta * delta), GAIN_MAX)
        guess = gain * (2.0 * guess - dot3(parts, halves(image)))
        return guess, 1.0 - gain * (1.0 - delta * delta)

    guess, _ = lax.fori_loop(0, steps, step, (start, 1.0 - 2.0 * lower / total))
    parts = thirds(guess)
    return 2.0 * guess - dot6(parts, thirds(dot6(block_parts, parts)))


def solve_kernel(rows_ref, out_ref, gram_ref, sys_ref, high_ref, low_ref):
    layers, slots, width = rows_ref.shape
    count = width // BLK

    def span(index):
        return pl.ds(pl.multiple_of(index * BLK, BLK), BLK)

    def gram_block(index, carry):
        layer, i, j = index // (count * count), index // count % count, index % count
        gram_ref[layer, span(i), span(j)] = lax.dot_general(
            rows_ref[layer, :, span(i)],
            rows_ref[layer, :, span(j)],
            (((0,), (0,)), ((), ())),
            preferred_element_type=F32,
        )
        return carry

    lax.fori_loop(0, layers * count * count, gram_block, 0)
    diag = lax.broadcasted_iota(jnp.int32, (BLK, BLK), 0) == lax.broadcasted_iota(
        jnp.int32, (BLK, BLK), 1
    )
    trace = jnp.float32(0)
    for i in range(count):
        here = slice(i * BLK, (i + 1) * BLK)
        block = gram_ref[0, here, here] + gram_ref[1, here, here] + gram_ref[2, here, here]
        trace = trace + jnp.sum(jnp.where(diag, block, 0.0))
    ridge = damping * trace / width + epsilon

    def system_block(i, carry):
        value = gram_ref[0, span(i), :] + gram_ref[1, span(i), :] + gram_ref[2, span(i), :]
        shape = (BLK, width)
        on = lax.broadcasted_iota(jnp.int32, shape, 0) + i * BLK == lax.broadcasted_iota(
            jnp.int32, shape, 1
        )
        sys_ref[span(i), :] = value + jnp.where(on, ridge, 0.0)
        return carry

    lax.fori_loop(0, count, system_block, 0)

    def sweep(k, carry):
        inverse = block_inverse(sys_ref[span(k), span(k)], ridge)
        inverse_parts = thirds(inverse)
        panel = dot6(inverse_parts, thirds(sys_ref[span(k), :]))
        panel_parts = thirds(panel)

        def eliminate(i, inner):
            @pl.when(i != k)
            def _():
                left = thirds(sys_ref[span(i), span(k)])
                sys_ref[span(i), :] = sys_ref[span(i), :] - dot6(left, panel_parts)
                sys_ref[span(i), span(k)] = dot6(left, inverse_parts)

            return inner

        lax.fori_loop(0, count, eliminate, 0)
        sys_ref[span(k), :] = panel
        sys_ref[span(k), span(k)] = -inverse
        return carry

    lax.fori_loop(0, count, sweep, 0)

    def split_gram(i, carry):
        for layer in range(1, layers):
            high, low = halves(gram_ref[layer, span(i), :])
            high_ref[layer - 1, span(i), :] = high
            low_ref[layer - 1, span(i), :] = low
        return carry

    lax.fori_loop(0, count, split_gram, 0)

    def member_block(index, carry):
        i, j = index // count, index % count
        inverse = halves(-sys_ref[span(i), :])
        first = dot3(inverse, (high_ref[0, :, span(j)], low_ref[0, :, span(j)]))
        second = dot3(inverse, (high_ref[1, :, span(j)], low_ref[1, :, span(j)]))
        rest = ridge * sys_ref[span(i), span(j)] - first - second
        rest = rest + jnp.where(diag & (i == j), 1.0, 0.0)
        out_ref[0, span(i), span(j)] = rest.astype(BF16)
        out_ref[1, span(i), span(j)] = first.astype(BF16)
        out_ref[2, span(i), span(j)] = second.astype(BF16)
        return carry

    lax.fori_loop(0, count * count, member_block, 0)


def member_maps(rows):
    layers, slots, width = rows.shape
    return pl.pallas_call(
        solve_kernel,
        out_shape=jax.ShapeDtypeStruct((layers, width, width), BF16),
        in_specs=[pl.BlockSpec(memory_space=pltpu.VMEM)],
        out_specs=pl.BlockSpec(memory_space=pltpu.VMEM),
        scratch_shapes=[
            pltpu.VMEM((layers, width, width), F32),
            pltpu.VMEM((width, width), F32),
            pltpu.VMEM((layers - 1, width, width), BF16),
            pltpu.VMEM((layers - 1, width, width), BF16),
        ],
        compiler_params=pltpu.CompilerParams(vmem_limit_bytes=56 * 1024 * 1024),
        cost_estimate=pl.CostEstimate(
            flops=40_000_000_000, bytes_accessed=12_000_000, transcendentals=0
        ),
        name="member_maps",
    )(rows)


CHUNK = 40


def pack_kernel(cap, routes_ref, column_ref, line_ref, rows_ref, out_ref):
    experts = column_ref.shape[0]
    count = routes_ref.shape[1]
    square = (experts, experts)
    earlier = lax.broadcasted_iota(jnp.int32, square, 1) < lax.broadcasted_iota(
        jnp.int32, square, 0
    )
    same = (column_ref[...] == line_ref[...]) & earlier
    rank = jnp.sum(jnp.where(same, 1.0, 0.0), axis=1, keepdims=True)
    base = column_ref[...].astype(F32) * CHUNK + rank * cap
    hit = lax.broadcasted_iota(jnp.int32, (experts, count), 0) == routes_ref[...]
    onehot = jnp.where(hit, 1.0, 0.0).astype(BF16)
    order = lax.broadcasted_iota(jnp.int32, (count, count), 0) < lax.broadcasted_iota(
        jnp.int32, (count, count), 1
    )
    before = dot(onehot, jnp.where(order, 1.0, 0.0).astype(BF16))
    slot = jnp.sum(jnp.where(hit, base + before, 0.0), axis=0, keepdims=True)
    slot = slot.astype(jnp.int32)

    def place(index, carry):
        here = pl.multiple_of(index * BLK, BLK)
        wanted = lax.broadcasted_iota(jnp.int32, (BLK, count), 0) + here
        pick = jnp.where(wanted == slot, 1.0, 0.0).astype(BF16)
        out_ref[pl.ds(here, BLK), :] = dot(pick, rows_ref[...]).astype(BF16)
        return carry

    lax.fori_loop(0, out_ref.shape[0] // BLK, place, 0)


def pack_rows(routes, merge_group, rows, cap, group_count):
    count, width = rows.shape
    experts = merge_group.shape[0]
    return pl.pallas_call(
        lambda *refs: pack_kernel(cap, *refs),
        out_shape=jax.ShapeDtypeStruct((group_count * CHUNK, width), BF16),
        in_specs=[pl.BlockSpec(memory_space=pltpu.VMEM)] * 4,
        out_specs=pl.BlockSpec(memory_space=pltpu.VMEM),
        compiler_params=pltpu.CompilerParams(vmem_limit_bytes=32 * 1024 * 1024),
        cost_estimate=pl.CostEstimate(
            flops=2_000_000_000, bytes_accessed=2_000_000, transcendentals=0
        ),
        name="pack_rows",
    )(routes.reshape(1, count), merge_group[:, None], merge_group[None, :], rows)


def pick_kernel(members_ref, pieces_ref, out_ref):
    groups, layers = out_ref.shape[:2]
    first = pl.program_id(0) * groups

    def copy_group(index, carry):
        for layer in range(layers):
            member = members_ref[(first + index) * layers + layer]
            out_ref[index, layer] = pieces_ref[member]
        return carry

    lax.fori_loop(0, groups, copy_group, 0)


def pick_members(pieces, members, group_count):
    experts, depth, width = pieces.shape
    part = group_count // 4
    return pl.pallas_call(
        pick_kernel,
        out_shape=jax.ShapeDtypeStruct((group_count, GMAX, depth, width), BF16),
        grid_spec=pltpu.PrefetchScalarGridSpec(
            num_scalar_prefetch=1,
            grid=(4,),
            in_specs=[pl.BlockSpec((experts, depth, width), lambda i, m: (0, 0, 0))],
            out_specs=pl.BlockSpec((part, GMAX, depth, width), lambda i, m: (i, 0, 0, 0)),
        ),
        compiler_params=pltpu.CompilerParams(vmem_limit_bytes=32 * 1024 * 1024),
        cost_estimate=pl.CostEstimate(
            flops=0, bytes_accessed=9_200_000, transcendentals=0
        ),
        name="pick_members",
    )(members, pieces)


def merge_kernel(maps_ref, weights_ref, out_ref, total_ref):
    layer = pl.program_id(0)
    groups, depth, width = weights_ref.shape
    size = out_ref.shape[0]

    def strip(index, carry):
        here = pl.ds(pl.multiple_of(index * BLK, BLK), BLK)
        weights = weights_ref[...].reshape(groups * depth, width)
        value = dot(maps_ref[here, :], weights)

        @pl.when(layer == 0)
        def _():
            total_ref[here, :] = value

        @pl.when(layer == 1)
        def _():
            total_ref[here, :] = total_ref[here, :] + value

        @pl.when(layer == 2)
        def _():
            out_ref[here, :] = (total_ref[here, :] + value).astype(BF16)

        return carry

    lax.fori_loop(0, size // BLK, strip, 0)


def merge_weights(maps, weights):
    layers, size, _ = maps.shape
    groups, _, depth, width = weights.shape
    return pl.pallas_call(
        merge_kernel,
        out_shape=jax.ShapeDtypeStruct((size, width), BF16),
        grid=(layers,),
        in_specs=[
            pl.BlockSpec((None, size, size), lambda l: (l, 0, 0)),
            pl.BlockSpec((groups, None, depth, width), lambda l: (0, l, 0, 0)),
        ],
        out_specs=pl.BlockSpec((size, width), lambda l: (0, 0)),
        scratch_shapes=[pltpu.VMEM((size, width), F32)],
        compiler_params=pltpu.CompilerParams(vmem_limit_bytes=40 * 1024 * 1024),
        cost_estimate=pl.CostEstimate(
            flops=5_600_000_000, bytes_accessed=13_000_000, transcendentals=0
        ),
        name="merge_weights",
    )(maps, weights)


def member_table(merge_group, group_count):
    experts = merge_group.shape[0]
    index = jnp.arange(experts, dtype=jnp.int32)
    earlier = index[None, :] < index[:, None]
    rank = jnp.sum((merge_group[:, None] == merge_group[None, :]) & earlier, axis=1)
    place = merge_group * GMAX + rank
    wanted = jnp.arange(group_count * GMAX, dtype=jnp.int32)
    return jnp.sum(jnp.where(place[None, :] == wanted[:, None], index[None, :], 0), axis=1)


def on_device(routes, routed_hidden, down_proj, merge_group):
    group_count = lax.axis_size("expert")
    local_count, full_width, out_part = down_proj.shape
    tok_count, top_count, hidden_part = routed_hidden.shape
    row_count = tok_count * top_count
    experts = merge_group.shape[0]
    cap = 3 * row_count // (2 * experts)
    depth = full_width // group_count

    pieces = down_proj.reshape(local_count, group_count, depth, out_part)
    pieces = lax.all_to_all(
        pieces.transpose(1, 0, 2, 3), "expert", split_axis=0, concat_axis=0, tiled=True
    )
    rows = routed_hidden.reshape(row_count, hidden_part)
    packed = pack_rows(routes, merge_group, rows, cap, group_count)
    packed = packed.reshape(group_count, CHUNK, hidden_part)
    arrived = lax.all_to_all(packed, "expert", split_axis=0, concat_axis=0, tiled=True)
    arrived = arrived[:, : GMAX * cap].reshape(group_count, GMAX, cap, hidden_part)
    arrived = arrived.transpose(1, 0, 2, 3).reshape(GMAX, group_count * cap, hidden_part)
    member_rows = lax.all_gather(arrived, "mp", axis=2, tiled=True)

    members = member_table(merge_group, group_count)
    picked = pick_members(
        pieces.reshape(experts, depth, out_part), members, group_count
    )
    weights = lax.all_to_all(picked, "expert", split_axis=0, concat_axis=0, tiled=True)
    maps = member_maps(member_rows)
    merged = merge_weights(maps, weights)
    return merged.reshape(1, full_width, out_part)


def solution(mesh):
    return jax.shard_map(
        on_device,
        mesh=mesh,
        in_specs=(P("expert", None), P("expert", None, "mp"), P("expert", None, "mp"), P()),
        out_specs=P("expert", None, "mp"),
        check_vma=False,
    )
```

time: 615 us -> 322 us (0.52); the launches traced: 605 us -> 322 us
  other arithmetic: 278 us -> 0.3 us
  Pallas kernels: 0 us -> 103 us
  matrix products: 82.2 us -> 0 us
  local copies, waits for them, and re-layouts: 81.4 us -> 11.8 us
  waiting for transfers between devices: 117 us -> 168 us
  between operations: 20.3 us -> 13.5 us
    another operation x37 -> x0, other arithmetic: 265 us -> none  [the longest x30 181 us: solve_group(): factor = jnp.linalg.cholesky(system)]
    pallas_call x0 -> x4, Pallas kernels: none -> 103 us  [the longest x1 83 us: member_maps(): pl.pallas_call(solve_kernel, out_shape=jax.ShapeDtypeStruct((layers, widt...]
    all_gather x1, waiting for transfers between devices: 0.02 us -> 59.7 us  [on_device(): member_rows = lax.all_gather(arrived, 'mp', axis=2, tiled=True)]
    another operation x44 -> x0, matrix products: 54.5 us -> none  [the longest x30 31.3 us: solve_group(): return jax.scipy.linalg.cho_solve((factor, True), partial_value)]
    dot_general x2 -> x0, matrix products: 27.8 us -> none  [the longest x1 17.1 us: member_work(): jnp.einsum('rsf,rsd->fd', member_rows, projected, preferred_element_type=...]
    gather x4 -> x0, local copies, waits for them, and re-layouts: 26.6 us -> none  [the longest x1 6.86 us: on_device(): padded[source_row]]
    another operation x38 -> x0, local copies, waits for them, and re-layouts: 25.5 us -> none
    all_to_all x3, waiting for transfers between devices: 117 us -> 108 us  [the longest x1 79.8 us: on_device(): lax.all_to_all(pieces.transpose(1, 0, 2, 3), 'expert', split_axis=0, conc...]
  transfers between devices with their start and end apart: 4 -> 4, of which waited for: 2 -> 3; matrix products, arithmetic and copies ran while one was open for 58% -> 1% of each run, Pallas kernels for 0% -> 28%
where the time goes in v1:
time: 322 us
  waiting for transfers between devices  168 us (52%)
  Pallas kernels  103 us (32%)
  starting transfers between devices  25.4 us (8%)
  between operations  13.5 us (4%)
  local copies, waits for them, and re-layouts  11.8 us (4%)
    pallas_call x1, Pallas kernels, member_maps(): pl.pallas_call(solve_kernel, out_shape=jax.ShapeDtypeStruct((layers, widt...  83 us
    all_to_all x1, waiting for transfers between devices, on_device(): lax.all_to_all(pieces.transpose(1, 0, 2, 3), 'expert', split_axis=0, conc...  79.8 us
    all_gather x1, waiting for transfers between devices, on_device(): member_rows = lax.all_gather(arrived, 'mp', axis=2, tiled=True)  59.7 us
    all_to_all x1, waiting for transfers between devices, on_device(): lax.all_to_all(packed, 'expert', split_axis=0, concat_axis=0, tiled=True)  28 us
    all_to_all x1, starting transfers between devices, on_device(): lax.all_to_all(pieces.transpose(1, 0, 2, 3), 'expert', split_axis=0, conc...  13.3 us
    pallas_call x1, Pallas kernels, merge_weights(): pl.pallas_call(merge_kernel, out_shape=jax.ShapeDtypeStruct((size, width)...  12.4 us
  transfers between devices with their start and end apart: 4, of which 3 were waited for; matrix products, arithmetic and copies ran while one was open for 1% of the time, Pallas kernels for 28%

profile of v1, /device:TPU:1, one launch (start us, length us, event | category | flops | bytes accessed | tf_op | source)
XLA Modules:
  0.0 322.0 jit_solution(14603682018672509960)
XLA Ops:
  6.5 4.2 %copy.25 = bf16[2,64,16,896]{3,2,0,1:T(8,128)(2,1)} copy(bf16[2,64,16,896]{3,2,1,0:T(8,128)(2,1)} %bitcast.20) | data formatting | bytes 7340032 | tf_op jit(solution)/shard_map/reshape | solution.py:338
  10.7 0.0 copy-start.4
  10.7 0.0 copy-start.1
  10.7 0.0 copy-start.2
  10.7 13.3 %all-to-all-start.1 = ((bf16[64,2,16,896]{3,2,1,0:T(8,128)(2,1)}), bf16[64,2,16,896]{3,2,1,0:T(8,128)(2,1)}, u32[]{:S(2)}, u32[]{:S(2)}) async-start(bf16[64,2,16,896]{3,2,1,0:T(8,128)(2,1)} %bitcast.17), calls=%async_computation.1 | async-start | bytes 7340032 | tf_op jit(solution)/shard_map/all_to_all | solution.py:339
  24.0 0.0 copy-done.4
  24.0 0.1 copy.18
  24.1 0.1 reshape.27.refs_0_
  24.2 0.0 copy-done.1
  24.2 0.1 copy.19.refs_1_
  24.4 0.0 copy-done.2
  24.4 4.6 %pack_rows.1 = bf16[2560,256]{1,0:T(8,128)(2,1)} custom-call(s32[1,1024]{1,0:T(1,128)S(1)} %reshape.27.refs_0_, s32[128,1]{1,0:T(8,128)S(1)} %copy.19.refs_1_, s32[1,128]{1,0:T(1,128)S(1)} %bitcast.15, bf16[1024,256]{1,0:T(8,128)(2,1)S(1)} %bitcast.16), custom_call_target="tpu_custom_call" | custom-call | flops 2000000000 | bytes 2000000 | tf_op jit(solution)/shard_map/pack_rows/pallas_call | solution.py:225
  28.9 79.8 %all-to-all-done.1 = bf16[64,2,16,896]{3,2,1,0:T(8,128)(2,1)} async-done(((bf16[64,2,16,896]{3,2,1,0:T(8,128)(2,1)}), bf16[64,2,16,896]{3,2,1,0:T(8,128)(2,1)}, u32[]{:S(2)}, u32[]{:S(2)}) %all-to-all-start.1) | async-done | bytes 3670048 | tf_op jit(solution)/shard_map/all_to_all | solution.py:339
  108.7 5.7 %all-to-all-start = ((bf16[64,40,256]{2,1,0:T(8,128)(2,1)}), bf16[64,40,256]{2,1,0:T(8,128)(2,1)S(1)}, u32[]{:S(2)}, u32[]{:S(2)}) async-start(bf16[64,40,256]{2,1,0:T(8,128)(2,1)} %bitcast.3), calls=%async_computation | async-start | bytes 2621440 | tf_op jit(solution)/shard_map/all_to_all | solution.py:345
  114.4 0.2 convert_reduce_fusion
  114.6 0.1 select_reduce_fusion.members_ref
  114.8 3.5 %pick_members.1 = bf16[64,3,16,896]{3,2,1,0:T(8,128)(2,1)S(1)} custom-call(s32[192]{0:T(256)S(1)} %select_reduce_fusion.members_ref, bf16[128,16,896]{2,1,0:T(8,128)(2,1)} %bitcast.8.pieces_ref), custom_call_target="tpu_custom_call" | custom-call | bytes 9200000 | tf_op jit(solution)/shard_map/pick_members/pallas_call | solution.py:254
  118.3 0.0 copy-start
  118.3 2.4 copy-done
  120.6 28.0 %all-to-all-done = bf16[64,40,256]{2,1,0:T(8,128)(2,1)S(1)} async-done(((bf16[64,40,256]{2,1,0:T(8,128)(2,1)}), bf16[64,40,256]{2,1,0:T(8,128)(2,1)S(1)}, u32[]{:S(2)}, u32[]{:S(2)}) %all-to-all-start) | async-done | bytes 1310752 | tf_op jit(solution)/shard_map/all_to_all | solution.py:345
  148.6 6.3 %all-to-all-start.2 = ((bf16[64,3,16,896]{3,2,1,0:T(8,128)(2,1)}), bf16[64,3,16,896]{3,2,1,0:T(8,128)(2,1)}, u32[]{:S(2)}, u32[]{:S(2)}) async-start(bf16[64,3,16,896]{3,2,1,0:T(8,128)(2,1)} %copy-done), calls=%async_computation.2 | async-start | bytes 11010048 | tf_op jit(solution)/shard_map/all_to_all | solution.py:354
  155.0 0.0 all-gather.2.cloned.1.call-start
  155.0 0.3 copy.23
  155.3 0.7 copy.21
  156.0 1.2 reshape.31
  157.1 0.0 all-gather.2.cloned.1.call-update
  157.2 59.7 %all-gather.2.cloned.1.call-done.rows_ref = bf16[3,768,1024]{2,1,0:T(8,128)(2,1)} async-done(((bf16[3,768,256]{2,1,0:T(8,128)(2,1)}), bf16[3,768,1024]{2,1,0:T(8,128)(2,1)}) %all-gather.2.cloned.1.call-update) | async-done | bytes 4718608 | tf_op jit(solution)/shard_map/all_gather | solution.py:348
  216.9 83.0 %member_maps.1.maps_ref = bf16[3,1024,1024]{2,1,0:T(8,128)(2,1)} custom-call(bf16[3,768,1024]{2,1,0:T(8,128)(2,1)} %all-gather.2.cloned.1.call-done.rows_ref), custom_call_target="tpu_custom_call" | custom-call | flops 40000000000 | bytes 12000000 | tf_op jit(solution)/shard_map/member_maps/pallas_call | solution.py:171
  299.9 0.0 all-to-all-done.2.weights_ref
  299.9 0.0 copy-start.3
  299.9 2.8 copy-done.3
  302.7 12.4 %merge_weights.1 = bf16[1024,896]{1,0:T(8,128)(2,1)} custom-call(bf16[3,1024,1024]{2,1,0:T(8,128)(2,1)S(1)} %copy-done.3, bf16[64,3,16,896]{3,2,1,0:T(8,128)(2,1)} %all-to-all-done.2.weights_ref), custom_call_target="tpu_custom_call" | custom-call | flops 5600000000 | bytes 13000000 | tf_op jit(solution)/shard_map/merge_weights/pallas_call | solution.py:301
  (1 shorter events, 0.0 us)
Async XLA Ops:
  10.7 13.3 %copy-start.4 = (s32[128,8]{0,1:T(8,128)S(1)}, s32[128,8]{0,1:T(8,128)}, u32[]{:S(2)}) copy-start(s32[128,8]{0,1:T(8,128)} %param.4) | copy-start | bytes 12292
  10.7 13.5 %copy-start.1 = (s32[128]{0:T(128)S(1)}, s32[128]{0:T(128)}, u32[]{:S(2)}) copy-start(s32[128]{0:T(128)} %param.7) | copy-start | bytes 1540
  10.7 13.6 %copy-start.2 = (bf16[128,8,256]{2,1,0:T(8,128)(2,1)S(1)}, bf16[128,8,256]{2,1,0:T(8,128)(2,1)}, u32[]{:S(2)}) copy-start(bf16[128,8,256]{2,1,0:T(8,128)(2,1)} %param.5) | copy-start | bytes 1572868
  10.7 98.0 %all-to-all-start.1 = ((bf16[64,2,16,896]{3,2,1,0:T(8,128)(2,1)}), bf16[64,2,16,896]{3,2,1,0:T(8,128)(2,1)}, u32[]{:S(2)}, u32[]{:S(2)}) async-start(bf16[64,2,16,896]{3,2,1,0:T(8,128)(2,1)} %bitcast.17), calls=%async_computation.1 | async-start | bytes 7340032 | tf_op jit(solution)/shard_map/all_to_all | solution.py:339
  108.7 39.9 %all-to-all-start = ((bf16[64,40,256]{2,1,0:T(8,128)(2,1)}), bf16[64,40,256]{2,1,0:T(8,128)(2,1)S(1)}, u32[]{:S(2)}, u32[]{:S(2)}) async-start(bf16[64,40,256]{2,1,0:T(8,128)(2,1)} %bitcast.3), calls=%async_computation | async-start | bytes 2621440 | tf_op jit(solution)/shard_map/all_to_all | solution.py:345
  118.3 2.4 copy-start
  148.6 151.3 %all-to-all-start.2 = ((bf16[64,3,16,896]{3,2,1,0:T(8,128)(2,1)}), bf16[64,3,16,896]{3,2,1,0:T(8,128)(2,1)}, u32[]{:S(2)}, u32[]{:S(2)}) async-start(bf16[64,3,16,896]{3,2,1,0:T(8,128)(2,1)} %copy-done), calls=%async_computation.2 | async-start | bytes 11010048 | tf_op jit(solution)/shard_map/all_to_all | solution.py:354
  155.0 62.0 %all-gather.2.cloned.1.call-start = ((), (), s32[]{:S(2)}) async-start(), calls=%async_computation.3 | async-start | bytes 5898240 | tf_op jit(solution)/shard_map/all_gather | solution.py:348
  299.9 2.8 copy-start.3
Sparse Core Ops, SparseCore 0:
  157.6 59.2 all-gather.1

commit v2 on v0

v2 whole, which is shorter than its diff:
```python
import jax
import jax.numpy as jnp
from jax import lax
from jax.experimental import pallas as pl
from jax.experimental.pallas import tpu as pltpu
from jax.sharding import PartitionSpec as P

GMAX = 3
BLK = 256
damping = 0.1
epsilon = 1e-05
F32 = jnp.float32
BF16 = jnp.bfloat16


def sweep_counts():
    gaps, delta = [], 1e-3
    for _ in range(16):
        gaps.append(1.0 - delta)
        if 2.0 * delta / (1.0 + delta) > 2.0 - 2.0 / GAIN_MAX:
            delta = (1.0 - (1.0 - delta) / GAIN_MAX) ** 0.5
        else:
            delta = (2.0 * delta / (1.0 + delta)) ** 0.5
    return gaps


GAIN_MAX = 1.85
NEWTON_GAPS = sweep_counts()


def halves(value):
    high = value.astype(BF16)
    return high, (value - high.astype(F32)).astype(BF16)


def dot(a, b):
    return jnp.dot(a, b, preferred_element_type=F32)


def dot3(a, b):
    (ah, al), (bh, bl) = a, b
    return dot(ah, bh) + (dot(ah, bl) + dot(al, bh))


def thirds(value):
    high = value.astype(BF16)
    rest = value - high.astype(F32)
    mid = rest.astype(BF16)
    return high, mid, (rest - mid.astype(F32)).astype(BF16)


def dot6(a, b):
    (ah, am, al), (bh, bm, bl) = a, b
    small = dot(am, bm) + (dot(ah, bl) + dot(al, bh))
    return dot(ah, bh) + (dot(ah, bm) + dot(am, bh) + small)


def block_inverse(block, lower):
    size = block.shape[0]
    upper = jnp.max(jnp.sum(jnp.abs(block), axis=1, keepdims=True))
    gap = 2.0 * lower / (lower + upper)
    steps = jnp.int32(0)
    for edge in NEWTON_GAPS:
        steps = steps + (gap < edge).astype(jnp.int32)
    rows = lax.broadcasted_iota(jnp.int32, (size, size), 0)
    cols = lax.broadcasted_iota(jnp.int32, (size, size), 1)
    total = jnp.full((1, size), lower + upper, F32)
    start = jnp.where(rows == cols, 2.0 / total, 0.0)
    block_parts = thirds(block)

    def step(_, carry):
        guess, delta = carry
        parts = halves(guess)
        image = dot3(block_parts[:2], parts)
        gain = jnp.minimum(2.0 / (2.0 - delta * delta), GAIN_MAX)
        guess = gain * (2.0 * guess - dot3(parts, halves(image)))
        return guess, 1.0 - gain * (1.0 - delta * delta)

    guess, _ = lax.fori_loop(0, steps, step, (start, 1.0 - 2.0 * lower / total))
    parts = thirds(guess)
    return 2.0 * guess - dot6(parts, thirds(dot6(block_parts, parts)))


TILE = 8
HELD = 3
OWNED = 5


def slot_kernel(routes_ref, bases_ref, rows_ref, out_ref, slot_ref):
    experts = bases_ref.shape[0]
    count = routes_ref.shape[1]
    hit = lax.broadcasted_iota(jnp.int32, (experts, count), 0) == routes_ref[...]
    onehot = jnp.where(hit, 1.0, 0.0).astype(BF16)
    order = lax.broadcasted_iota(jnp.int32, (count, count), 0) < lax.broadcasted_iota(
        jnp.int32, (count, count), 1
    )
    before = dot(onehot, jnp.where(order, 1.0, 0.0).astype(BF16))
    bases = bases_ref[...].astype(F32)
    place = before + jnp.where(before < TILE, bases[:, 0:1], bases[:, 1:2])
    slot = jnp.sum(jnp.where(hit, place, 0.0), axis=0, keepdims=True)
    slot_ref[...] = slot.astype(jnp.int32)

    def fill(index, carry):
        here = pl.multiple_of(index * BLK, BLK)
        wanted = lax.broadcasted_iota(jnp.int32, (BLK, count), 0) + here
        pick = jnp.where(wanted == slot_ref[...], 1.0, 0.0).astype(BF16)
        out_ref[pl.ds(here, BLK), :] = dot(pick, rows_ref[...]).astype(BF16)
        return carry

    lax.fori_loop(0, out_ref.shape[0] // BLK, fill, 0)


def pack_rows(routes, bases, rows, slots, name):
    count, width = rows.shape
    return pl.pallas_call(
        slot_kernel,
        out_shape=jax.ShapeDtypeStruct((slots, width), BF16),
        in_specs=[pl.BlockSpec(memory_space=pltpu.VMEM)] * 3,
        out_specs=pl.BlockSpec(memory_space=pltpu.VMEM),
        scratch_shapes=[pltpu.VMEM((1, count), jnp.int32)],
        compiler_params=pltpu.CompilerParams(vmem_limit_bytes=32 * 1024 * 1024),
        cost_estimate=pl.CostEstimate(
            flops=3_000_000_000, bytes_accessed=2_000_000, transcendentals=0
        ),
        name=name,
    )(routes, bases, rows)


def project_kernel(rows_ref, weights_ref, out_ref):
    parts, blocks = rows_ref.shape[:2]
    width = out_ref.shape[3]
    step = BLK // TILE
    upper = lax.broadcasted_iota(jnp.int32, (BLK, 1), 0) % TILE < TILE // 2

    def strip(index, carry):
        here = pl.ds(index * step, step)
        for tile in range(HELD):
            rows = jnp.concatenate(
                [rows_ref[m, here, tile].reshape(BLK, -1) for m in range(parts)], axis=1
            )
            if tile < 2:
                value = dot(rows, weights_ref[tile])
            else:
                none = jnp.zeros_like(rows)
                value = dot(jnp.where(upper, rows, none), weights_ref[0])
                value = value + dot(jnp.where(upper, none, rows), weights_ref[1])
            out_ref[here, tile] = value.astype(BF16).reshape(step, TILE, width)
        return carry

    lax.fori_loop(0, blocks // step, strip, 0)


def project_rows(rows, weights):
    blocks = rows.shape[1]
    width = weights.shape[2]
    return pl.pallas_call(
        project_kernel,
        out_shape=jax.ShapeDtypeStruct((blocks, HELD, TILE, width), BF16),
        in_specs=[pl.BlockSpec(memory_space=pltpu.VMEM)] * 2,
        out_specs=pl.BlockSpec(memory_space=pltpu.VMEM),
        compiler_params=pltpu.CompilerParams(vmem_limit_bytes=40 * 1024 * 1024),
        cost_estimate=pl.CostEstimate(
            flops=4_000_000_000, bytes_accessed=10_000_000, transcendentals=0
        ),
        name="project_rows",
    )(rows, weights)


def regroup_kernel(members_ref, held_ref, out_ref):
    groups = out_ref.shape[0]
    first = pl.program_id(0) * groups
    width = out_ref.shape[3]
    upper = lax.broadcasted_iota(jnp.int32, (TILE, width), 0) < TILE // 2

    def regroup(index, carry):
        ends = []
        for layer in range(GMAX):
            member = members_ref[(first + index) * GMAX + layer]
            holder, local = member // 2, member % 2
            out_ref[index, layer] = held_ref[holder, local]
            end = held_ref[holder, 2].astype(F32)
            turned = pltpu.roll(end, TILE // 2, 0)
            ends.append(jnp.where(local == layer % 2, end, turned))
        out_ref[index, 3] = jnp.where(upper, ends[0], ends[1]).astype(BF16)
        out_ref[index, 4] = jnp.where(upper, ends[2], 0.0).astype(BF16)
        return carry

    lax.fori_loop(0, groups, regroup, 0)


def regroup_rows(held, members):
    group_count, _, _, width = held.shape
    part = group_count // 4
    return pl.pallas_call(
        regroup_kernel,
        out_shape=jax.ShapeDtypeStruct((group_count, OWNED, TILE, width), BF16),
        grid_spec=pltpu.PrefetchScalarGridSpec(
            num_scalar_prefetch=1,
            grid=(4,),
            in_specs=[pl.BlockSpec(held.shape, lambda i, m: (0, 0, 0, 0))],
            out_specs=pl.BlockSpec((part, OWNED, TILE, width), lambda i, m: (i, 0, 0, 0)),
        ),
        compiler_params=pltpu.CompilerParams(vmem_limit_bytes=32 * 1024 * 1024),
        cost_estimate=pl.CostEstimate(
            flops=0, bytes_accessed=7_500_000, transcendentals=0
        ),
        name="regroup_rows",
    )(members, held)


def invert_kernel(rows_ref, after_ref, high_ref, low_ref, turned_ref, sys_ref):
    del after_ref
    count, slots, _ = rows_ref.shape
    width = count * BLK
    diag = lax.broadcasted_iota(jnp.int32, (BLK, BLK), 0) == lax.broadcasted_iota(
        jnp.int32, (BLK, BLK), 1
    )

    def span(index):
        return pl.ds(pl.multiple_of(index * BLK, BLK), BLK)

    def turn(i, carry):
        turned_ref[span(i), :] = rows_ref[i].T
        return carry

    lax.fori_loop(0, count, turn, 0)

    def gram_block(index, carry):
        i, j = index // count, index % count
        sys_ref[span(i), span(j)] = dot(turned_ref[span(i), :], rows_ref[j])
        return carry

    lax.fori_loop(0, count * count, gram_block, 0)
    trace = jnp.float32(0)
    for i in range(count):
        here = slice(i * BLK, (i + 1) * BLK)
        trace = trace + jnp.sum(jnp.where(diag, sys_ref[here, here], 0.0))
    ridge = damping * trace / width + epsilon
    for i in range(count):
        here = slice(i * BLK, (i + 1) * BLK)
        sys_ref[here, here] = sys_ref[here, here] + jnp.where(diag, ridge, 0.0)

    def sweep(k, carry):
        inverse = block_inverse(sys_ref[span(k), span(k)], ridge)
        inverse_parts = thirds(inverse)
        panel = dot6(inverse_parts, thirds(sys_ref[span(k), :]))
        panel_parts = thirds(panel)

        def eliminate(i, inner):
            @pl.when(i != k)
            def _():
                left = thirds(sys_ref[span(i), span(k)])
                sys_ref[span(i), :] = sys_ref[span(i), :] - dot6(left, panel_parts)
                sys_ref[span(i), span(k)] = dot6(left, inverse_parts)

            return inner

        lax.fori_loop(0, count, eliminate, 0)
        sys_ref[span(k), :] = panel
        sys_ref[span(k), span(k)] = -inverse
        return carry

    lax.fori_loop(0, count, sweep, 0)

    def split(i, carry):
        high, low = halves(-sys_ref[span(i), :])
        high_ref[span(i), :] = high
        low_ref[span(i), :] = low
        return carry

    lax.fori_loop(0, count, split, 0)


def invert_gram(rows, after):
    count, slots, _ = rows.shape
    width = count * BLK
    square = jax.ShapeDtypeStruct((width, width), BF16)
    return pl.pallas_call(
        invert_kernel,
        out_shape=(square, square, jax.ShapeDtypeStruct((width, slots), BF16)),
        in_specs=[
            pl.BlockSpec(memory_space=pltpu.VMEM),
            pl.BlockSpec(memory_space=pl.ANY),
        ],
        out_specs=[pl.BlockSpec(memory_space=pltpu.VMEM)] * 3,
        scratch_shapes=[pltpu.VMEM((width, width), F32)],
        compiler_params=pltpu.CompilerParams(vmem_limit_bytes=40 * 1024 * 1024),
        cost_estimate=pl.CostEstimate(
            flops=60_000_000_000, bytes_accessed=16_000_000, transcendentals=0
        ),
        name="invert_gram",
    )(rows, after)


def merge_kernel(turned_ref, projected_ref, high_ref, low_ref, out_ref, first_ref, second_ref):
    size = out_ref.shape[0]

    def span(index):
        return pl.ds(pl.multiple_of(index * BLK, BLK), BLK)

    def gather(i, carry):
        high, low = halves(dot(turned_ref[span(i), :], projected_ref[...]))
        first_ref[span(i), :] = high
        second_ref[span(i), :] = low
        return carry

    lax.fori_loop(0, size // BLK, gather, 0)

    def strip(i, carry):
        inverse = (high_ref[span(i), :], low_ref[span(i), :])
        value = dot3(inverse, (first_ref[...], second_ref[...]))
        out_ref[span(i), :] = value.astype(BF16)
        return carry

    lax.fori_loop(0, size // BLK, strip, 0)


def merge_rows(turned, projected, high, low):
    size = turned.shape[0]
    width = projected.shape[1]
    return pl.pallas_call(
        merge_kernel,
        out_shape=jax.ShapeDtypeStruct((size, width), BF16),
        in_specs=[pl.BlockSpec(memory_space=pltpu.VMEM)] * 4,
        out_specs=pl.BlockSpec(memory_space=pltpu.VMEM),
        scratch_shapes=[pltpu.VMEM((size, width), BF16)] * 2,
        compiler_params=pltpu.CompilerParams(vmem_limit_bytes=40 * 1024 * 1024),
        cost_estimate=pl.CostEstimate(
            flops=10_300_000_000, bytes_accessed=16_000_000, transcendentals=0
        ),
        name="merge_rows",
    )(turned, projected, high, low)


def member_places(merge_group, group_count):
    experts = merge_group.shape[0]
    index = jnp.arange(experts, dtype=jnp.int32)
    earlier = index[None, :] < index[:, None]
    rank = jnp.sum(
        (merge_group[:, None] == merge_group[None, :]) & earlier, axis=1, dtype=jnp.int32
    )
    place = merge_group * GMAX + rank
    wanted = jnp.arange(group_count * GMAX, dtype=jnp.int32)
    members = jnp.sum(jnp.where(place[None, :] == wanted[:, None], index[None, :], 0), axis=1)
    chunk = merge_group * (OWNED * TILE)
    bases = [chunk + rank * TILE, chunk + GMAX * TILE + rank * (TILE // 2) - TILE]
    return members, jnp.stack(bases, axis=1)


def exchange(rows):
    return lax.all_to_all(rows, "expert", split_axis=0, concat_axis=0, tiled=True)


def on_device(routes, routed_hidden, down_proj, merge_group):
    group_count = lax.axis_size("expert")
    parts = lax.axis_size("mp")
    full_width, out_part = down_proj.shape[1:]
    tok_count, top_count, hidden_part = routed_hidden.shape
    row_count = tok_count * top_count
    experts = merge_group.shape[0]

    rows = routed_hidden.reshape(row_count, hidden_part)
    targets = routes.reshape(1, row_count)
    index = jnp.arange(experts, dtype=jnp.int32)
    chunk, local = index // 2 * (HELD * TILE), index % 2
    held_bases = jnp.stack(
        [chunk + local * TILE, chunk + 2 * TILE + local * (TILE // 2) - TILE], axis=1
    )
    members, owned_bases = member_places(merge_group, group_count)

    to_holder = pack_rows(
        targets, held_bases, rows, group_count * HELD * TILE, "pack_held"
    ).reshape(group_count, HELD * TILE, hidden_part)
    to_owner = pack_rows(
        targets, owned_bases, rows, group_count * OWNED * TILE, "pack_owned"
    ).reshape(group_count, OWNED * TILE, hidden_part)
    at_holder = exchange(to_holder)
    at_holder, to_owner = lax.optimization_barrier((at_holder, to_owner))
    held = lax.all_gather(at_holder, "mp", axis=0)
    at_owner = exchange(to_owner)

    projected = project_rows(
        held.reshape(parts, group_count, HELD, TILE, hidden_part), down_proj
    )
    at_owner, projected = lax.optimization_barrier((at_owner, projected))
    home = exchange(projected.reshape(group_count, HELD * TILE, out_part))
    owned = lax.all_gather(at_owner, "mp", axis=0)
    regrouped = regroup_rows(home.reshape(group_count, HELD, TILE, out_part), members)
    regrouped = regrouped.reshape(group_count, OWNED * TILE, out_part)
    arrived = exchange(regrouped)

    slots = group_count * OWNED * TILE
    high, low, turned = invert_gram(owned.reshape(parts, slots, hidden_part), regrouped)
    merged = merge_rows(turned, arrived.reshape(slots, out_part), high, low)
    return merged.reshape(1, full_width, out_part)


def solution(mesh):
    return jax.shard_map(
        on_device,
        mesh=mesh,
        in_specs=(P("expert", None), P("expert", None, "mp"), P("expert", None, "mp"), P()),
        out_specs=P("expert", None, "mp"),
        check_vma=False,
    )
```

time: 615 us -> 319 us (0.52); the launches traced: 605 us -> 318 us
  other arithmetic: 278 us -> 0.32 us
  Pallas kernels: 0 us -> 86.9 us
  matrix products: 82.2 us -> 0 us
  local copies, waits for them, and re-layouts: 81.4 us -> 21.8 us
  waiting for transfers between devices: 117 us -> 160 us
  starting transfers between devices: 25.6 us -> 35.8 us
  between operations: 20.3 us -> 13.6 us
    another operation x37 -> x2, other arithmetic: 265 us -> 0.02 us  [the longest x1 0.01 us: member_places(): return (members, jnp.stack(bases, axis=1))]
    pallas_call x0 -> x6, Pallas kernels: none -> 86.9 us  [the longest x1 54.6 us: invert_gram(): pl.pallas_call(invert_kernel, out_shape=(square, square, jax.ShapeDtypeSt...]
    another operation x44 -> x0, matrix products: 54.5 us -> none  [the longest x30 31.3 us: solve_group(): return jax.scipy.linalg.cho_solve((factor, True), partial_value)]
    all_gather x1 -> x2, waiting for transfers between devices: 0.02 us -> 33.1 us  [the longest x1 33.1 us: on_device(): held = lax.all_gather(at_holder, 'mp', axis=0)]
    dot_general x2 -> x0, matrix products: 27.8 us -> none  [the longest x1 17.1 us: member_work(): jnp.einsum('rsf,rsd->fd', member_rows, projected, preferred_element_type=...]
    gather x4 -> x0, local copies, waits for them, and re-layouts: 26.6 us -> none  [the longest x1 6.86 us: on_device(): padded[source_row]]
    another operation x38 -> x2, local copies, waits for them, and re-layouts: 25.5 us -> 0.23 us  [the longest x1 0.11 us: on_device(): jnp.stack([chunk + local * TILE, chunk + 2 * TILE + local * (TILE // 2) -...]
    unnamed x26 -> x29, local copies, waits for them, and re-layouts: 4.43 us -> 21.5 us
  transfers between devices with their start and end apart: 4 -> 6, of which waited for: 2 -> 4; matrix products, arithmetic and copies ran while one was open for 58% -> 0% of each run, Pallas kernels for 0% -> 21%
where the time goes in v2:
time: 319 us; the launch traced here: 318 us
  waiting for transfers between devices  160 us (50%)
  Pallas kernels  86.9 us (27%)
  starting transfers between devices  35.8 us (11%)
  local copies, waits for them, and re-layouts  21.8 us (7%)
  between operations  13.6 us (4%)
    all_to_all x4, waiting for transfers between devices, exchange(): lax.all_to_all(rows, 'expert', split_axis=0, concat_axis=0, tiled=True)  126 us
    pallas_call x1, Pallas kernels, invert_gram(): pl.pallas_call(invert_kernel, out_shape=(square, square, jax.ShapeDtypeSt...  54.6 us
    all_to_all x4, starting transfers between devices, exchange(): lax.all_to_all(rows, 'expert', split_axis=0, concat_axis=0, tiled=True)  35.8 us
    all_gather x1, waiting for transfers between devices, on_device(): held = lax.all_gather(at_holder, 'mp', axis=0)  33.1 us
    unnamed x29, local copies, waits for them, and re-layouts  21.5 us
    pallas_call x1, Pallas kernels, merge_rows(): pl.pallas_call(merge_kernel, out_shape=jax.ShapeDtypeStruct((size, width)...  16.9 us
    pallas_call x2, Pallas kernels, pack_rows(): pl.pallas_call(slot_kernel, out_shape=jax.ShapeDtypeStruct((slots, width)...  7.8 us
  transfers between devices with their start and end apart: 6, of which 4 were waited for; matrix products, arithmetic and copies ran while one was open for 0% of the time, Pallas kernels for 21%

profile of v2, /device:TPU:1, one launch (start us, length us, event | category | flops | bytes accessed | tf_op | source)
XLA Modules:
  0.0 318.1 jit_solution(9335812075052023692)
XLA Ops:
  6.5 0.8 copy.14
  7.4 0.1 copy.15.bases_ref
  7.6 1.0 copy-done.5
  8.6 3.2 %pack_held.1 = bf16[1536,256]{1,0:T(8,128)(2,1)} custom-call(s32[1,1024]{1,0:T(1,128)S(1)} %reshape.107.routes_ref, s32[128,2]{1,0:T(8,128)S(1)} %copy.15.bases_ref, bf16[1024,256]{1,0:T(8,128)(2,1)S(1)} %bitcast.19), custom_call_target="tpu_custom_call" | custom-call | flops 3000000000 | bytes 2000000 | tf_op jit(solution)/shard_map/pack_held/pallas_call | solution.py:115
  11.8 13.0 %all-to-all-start = ((bf16[64,24,256]{2,1,0:T(8,128)(2,1)}), bf16[64,24,256]{2,1,0:T(8,128)(2,1)S(1)}, u32[]{:S(2)}, u32[]{:S(2)}) async-start(bf16[64,24,256]{2,1,0:T(8,128)(2,1)} %bitcast.1), calls=%async_computation | async-start | bytes 1572864 | tf_op jit(solution)/shard_map/all_to_all | solution.py:351
  24.9 0.2 convert_reduce_fusion
  25.1 0.1 copy.16.bases_ref
  25.2 4.6 %pack_owned.1 = bf16[2560,256]{1,0:T(8,128)(2,1)} custom-call(s32[1,1024]{1,0:T(1,128)S(1)} %reshape.107.routes_ref, s32[128,2]{1,0:T(8,128)S(1)} %copy.16.bases_ref, bf16[1024,256]{1,0:T(8,128)(2,1)S(1)} %bitcast.20), custom_call_target="tpu_custom_call" | custom-call | flops 3000000000 | bytes 2000000 | tf_op jit(solution)/shard_map/pack_owned/pallas_call | solution.py:115
  29.8 18.0 %all-to-all-done = bf16[64,24,256]{2,1,0:T(8,128)(2,1)S(1)} async-done(((bf16[64,24,256]{2,1,0:T(8,128)(2,1)}), bf16[64,24,256]{2,1,0:T(8,128)(2,1)S(1)}, u32[]{:S(2)}, u32[]{:S(2)}) %all-to-all-start) | async-done | bytes 786464 | tf_op jit(solution)/shard_map/all_to_all | solution.py:351
  47.8 0.9 copy-done.12
  48.7 6.2 %all-to-all-start.1 = ((bf16[64,40,256]{2,1,0:T(8,128)(2,1)}), bf16[64,40,256]{2,1,0:T(8,128)(2,1)S(1)}, u32[]{:S(2)}, u32[]{:S(2)}) async-start(bf16[64,40,256]{2,1,0:T(8,128)(2,1)} %bitcast.4), calls=%async_computation.1 | async-start | bytes 2621440 | tf_op jit(solution)/shard_map/all_to_all | solution.py:351
  54.9 33.1 %all-gather.5.cloned.1.call-done = bf16[256,24,256]{2,1,0:T(8,128)(2,1)} async-done(((bf16[64,24,256]{2,1,0:T(8,128)(2,1)}), bf16[256,24,256]{2,1,0:T(8,128)(2,1)}) %all-gather.5.cloned.1.call-update) | async-done | bytes 3145744 | tf_op jit(solution)/shard_map/all_gather | solution.py:379
  88.0 2.0 copy-done.3
  90.0 1.9 copy-done.4
  91.9 4.7 %project_rows.1 = bf16[64,3,8,896]{3,2,1,0:T(8,128)(2,1)S(1)} custom-call(bf16[4,64,3,8,256]{4,3,2,1,0:T(8,128)(2,1)S(1)} %bitcast.18, bf16[2,1024,896]{2,1,0:T(8,128)(2,1)S(1)} %copy-done.3), custom_call_target="tpu_custom_call" | custom-call | flops 4000000000 | bytes 10000000 | tf_op jit(solution)/shard_map/project_rows/pallas_call | solution.py:156
  96.6 1.5 copy-done.2
  98.2 1.1 copy-done.11
  99.2 10.7 %all-to-all-start.2 = ((bf16[64,24,896]{2,1,0:T(8,128)(2,1)}), bf16[64,24,896]{2,1,0:T(8,128)(2,1)S(1)}, u32[]{:S(2)}, u32[]{:S(2)}) async-start(bf16[64,24,896]{2,1,0:T(8,128)(2,1)} %bitcast.17), calls=%async_computation.2 | async-start | bytes 5505024 | tf_op jit(solution)/shard_map/all_to_all | solution.py:351
  109.9 0.7 all-gather.7.cloned.1.call-update
  110.6 0.1 select_reduce_fusion.members_ref
  110.7 64.2 %all-to-all-done.2 = bf16[64,24,896]{2,1,0:T(8,128)(2,1)S(1)} async-done(((bf16[64,24,896]{2,1,0:T(8,128)(2,1)}), bf16[64,24,896]{2,1,0:T(8,128)(2,1)S(1)}, u32[]{:S(2)}, u32[]{:S(2)}) %all-to-all-start.2) | async-done | bytes 2752544 | tf_op jit(solution)/shard_map/all_to_all | solution.py:351
  175.0 3.0 regroup_rows.1
  177.9 2.2 copy-done
  180.1 5.9 %all-to-all-start.3 = ((bf16[64,40,896]{2,1,0:T(8,128)(2,1)}), bf16[64,40,896]{2,1,0:T(8,128)(2,1)}, u32[]{:S(2)}, u32[]{:S(2)}) async-start(bf16[64,40,896]{2,1,0:T(8,128)(2,1)} %bitcast.14), calls=%async_computation.3 | async-start | bytes 9175040 | tf_op jit(solution)/shard_map/all_to_all | solution.py:351
  186.1 2.3 copy-done.1
  188.4 54.6 %invert_gram.1 = (bf16[1024,1024]{1,0:T(8,128)(2,1)S(1)}, bf16[1024,1024]{1,0:T(8,128)(2,1)S(1)}, bf16[1024,2560]{1,0:T(8,128)(2,1)S(1)}) custom-call(bf16[4,2560,256]{2,1,0:T(8,128)(2,1)} %bitcast.21, bf16[64,40,896]{2,1,0:T(8,128)(2,1)S(1)} %bitcast.15), custom_call_target="tpu_custom_call" | custom-call | flops 60000002048 | bytes 16000000 | tf_op jit(solution)/shard_map/invert_gram/pallas_call | solution.py:278
  243.0 2.3 copy-done.7
  245.3 1.3 copy-done.9
  246.6 43.7 %all-to-all-done.3 = bf16[64,40,896]{2,1,0:T(8,128)(2,1)} async-done(((bf16[64,40,896]{2,1,0:T(8,128)(2,1)}), bf16[64,40,896]{2,1,0:T(8,128)(2,1)}, u32[]{:S(2)}, u32[]{:S(2)}) %all-to-all-start.3) | async-done | bytes 4587552 | tf_op jit(solution)/shard_map/all_to_all | solution.py:351
  290.4 2.5 copy-done.8
  292.9 1.6 copy-done.10
  294.4 16.9 %merge_rows.1 = bf16[1024,896]{1,0:T(8,128)(2,1)} custom-call(bf16[1024,2560]{1,0:T(8,128)(2,1)S(1)} %copy-done.8, bf16[2560,896]{1,0:T(8,128)(2,1)} %bitcast.10.projected_ref, bf16[1024,1024]{1,0:T(8,128)(2,1)S(1)} %get-tuple-element.17.high_ref, bf16[1024,1024]{1,0:T(8,128)(2,1)S(1)} %copy-done.10), custom_call_target="tpu_custom_call" | custom-call | flops 10300000256 | bytes 16000000 | tf_op jit(solution)/shard_map/merge_rows/pallas_call | solution.py:321
  (26 shorter events, 0.3 us)
Async XLA Ops:
  7.6 1.0 copy-start.5
  8.6 16.2 %copy-start.13 = (s32[128]{0:T(128)S(1)}, s32[128]{0:T(128)}, u32[]{:S(2)}) copy-start(s32[128]{0:T(128)} %param.7) | copy-start | bytes 1540
  8.6 16.6 %copy-start.6 = (bf16[128,8,256]{2,1,0:T(8,128)(2,1)S(1)}, bf16[128,8,256]{2,1,0:T(8,128)(2,1)}, u32[]{:S(2)}) copy-start(bf16[128,8,256]{2,1,0:T(8,128)(2,1)} %param.5) | copy-start | bytes 1572868
  11.8 36.0 %all-to-all-start = ((bf16[64,24,256]{2,1,0:T(8,128)(2,1)}), bf16[64,24,256]{2,1,0:T(8,128)(2,1)S(1)}, u32[]{:S(2)}, u32[]{:S(2)}) async-start(bf16[64,24,256]{2,1,0:T(8,128)(2,1)} %bitcast.1), calls=%async_computation | async-start | bytes 1572864 | tf_op jit(solution)/shard_map/all_to_all | solution.py:351
  24.8 63.2 %all-gather.5.cloned.1.call-start = ((), (), s32[]{:S(2)}) async-start(), calls=%async_computation.4 | async-start | bytes 3932160 | tf_op jit(solution)/shard_map/all_gather | solution.py:379
  47.8 0.9 copy-start.12
  48.7 49.5 %all-to-all-start.1 = ((bf16[64,40,256]{2,1,0:T(8,128)(2,1)}), bf16[64,40,256]{2,1,0:T(8,128)(2,1)S(1)}, u32[]{:S(2)}, u32[]{:S(2)}) async-start(bf16[64,40,256]{2,1,0:T(8,128)(2,1)} %bitcast.4), calls=%async_computation.1 | async-start | bytes 2621440 | tf_op jit(solution)/shard_map/all_to_all | solution.py:351
  88.0 2.0 copy-start.3
  90.0 1.9 copy-start.4
  96.6 1.5 copy-start.2
  98.2 1.1 copy-start.11
  99.2 75.7 %all-to-all-start.2 = ((bf16[64,24,896]{2,1,0:T(8,128)(2,1)}), bf16[64,24,896]{2,1,0:T(8,128)(2,1)S(1)}, u32[]{:S(2)}, u32[]{:S(2)}) async-start(bf16[64,24,896]{2,1,0:T(8,128)(2,1)} %bitcast.17), calls=%async_computation.2 | async-start | bytes 5505024 | tf_op jit(solution)/shard_map/all_to_all | solution.py:351
  109.9 76.2 %all-gather.7.cloned.1.call-start = ((), (), s32[]{:S(2)}) async-start(), calls=%async_computation.5 | async-start | bytes 6553600 | tf_op jit(solution)/shard_map/all_gather | solution.py:387
  177.9 2.2 copy-start
  180.1 110.2 %all-to-all-start.3 = ((bf16[64,40,896]{2,1,0:T(8,128)(2,1)}), bf16[64,40,896]{2,1,0:T(8,128)(2,1)}, u32[]{:S(2)}, u32[]{:S(2)}) async-start(bf16[64,40,896]{2,1,0:T(8,128)(2,1)} %bitcast.14), calls=%async_computation.3 | async-start | bytes 9175040 | tf_op jit(solution)/shard_map/all_to_all | solution.py:351
  186.1 2.3 copy-start.1
  243.0 2.3 copy-start.7
  245.3 1.3 copy-start.9
  290.4 2.5 copy-start.8
  292.9 1.6 copy-start.10
Sparse Core Ops, SparseCore 0:
  48.8 39.1 all-gather.4
  112.5 59.3 all-gather.6

commit v3 on v2

--- a/solution.py
+++ b/solution.py
@@ -84,6 +84,9 @@
 TILE = 8
 HELD = 3
 OWNED = 5
+KEPT = 4
+LANES = 128
+VMEM_GRANT = 58 * 1024 * 1024
 
 
 def slot_kernel(routes_ref, bases_ref, rows_ref, out_ref, slot_ref):
@@ -129,36 +132,40 @@
 def project_kernel(rows_ref, weights_ref, out_ref):
     parts, blocks = rows_ref.shape[:2]
     width = out_ref.shape[3]
-    step = BLK // TILE
-    upper = lax.broadcasted_iota(jnp.int32, (BLK, 1), 0) % TILE < TILE // 2
-
-    def strip(index, carry):
-        here = pl.ds(index * step, step)
-        for tile in range(HELD):
-            rows = jnp.concatenate(
-                [rows_ref[m, here, tile].reshape(BLK, -1) for m in range(parts)], axis=1
-            )
-            if tile < 2:
-                value = dot(rows, weights_ref[tile])
-            else:
-                none = jnp.zeros_like(rows)
-                value = dot(jnp.where(upper, rows, none), weights_ref[0])
-                value = value + dot(jnp.where(upper, none, rows), weights_ref[1])
-            out_ref[here, tile] = value.astype(BF16).reshape(step, TILE, width)
-        return carry
-
-    lax.fori_loop(0, blocks // step, strip, 0)
+    slots = blocks * TILE
+    upper = lax.broadcasted_iota(jnp.int32, (slots, 1), 0) % TILE < TILE // 2
+
+    def tile_rows(tile):
+        return jnp.concatenate(
+            [rows_ref[m, :, tile].reshape(slots, -1) for m in range(parts)], axis=1
+        )
+
+    ends = tile_rows(2)
+    none = jnp.zeros_like(ends)
+    mixed = None
+    for local in range(2):
+        end = jnp.where(upper, ends, none) if local == 0 else jnp.where(upper, none, ends)
+        rows = jnp.concatenate([tile_rows(local), end], axis=0)
+        value = dot(rows, weights_ref[local])
+        out_ref[:, local] = value[:slots].astype(BF16).reshape(blocks, TILE, width)
+        mixed = value[slots:] if mixed is None else mixed + value[slots:]
+    out_ref[:, 2] = mixed.astype(BF16).reshape(blocks, TILE, width)
 
 
 def project_rows(rows, weights):
-    blocks = rows.shape[1]
+    parts, blocks, _, _, hidden_part = rows.shape
     width = weights.shape[2]
+    step = 16
     return pl.pallas_call(
         project_kernel,
         out_shape=jax.ShapeDtypeStruct((blocks, HELD, TILE, width), BF16),
-        in_specs=[pl.BlockSpec(memory_space=pltpu.VMEM)] * 2,
-        out_specs=pl.BlockSpec(memory_space=pltpu.VMEM),
-        compiler_params=pltpu.CompilerParams(vmem_limit_bytes=40 * 1024 * 1024),
+        grid=(blocks // step,),
+        in_specs=[
+            pl.BlockSpec((parts, step, HELD, TILE, hidden_part), lambda i: (0, i, 0, 0, 0)),
+            pl.BlockSpec(weights.shape, lambda i: (0, 0, 0)),
+        ],
+        out_specs=pl.BlockSpec((step, HELD, TILE, width), lambda i: (i, 0, 0, 0)),
+        compiler_params=pltpu.CompilerParams(vmem_limit_bytes=VMEM_GRANT),
         cost_estimate=pl.CostEstimate(
             flops=4_000_000_000, bytes_accessed=10_000_000, transcendentals=0
         ),
@@ -169,20 +176,33 @@
 def regroup_kernel(members_ref, held_ref, out_ref):
     groups = out_ref.shape[0]
     first = pl.program_id(0) * groups
-    width = out_ref.shape[3]
+    width = held_ref.shape[3]
+    blocks = width // LANES
     upper = lax.broadcasted_iota(jnp.int32, (TILE, width), 0) < TILE // 2
+    upper_block = upper[:, :LANES]
+
+    def lanes(value, block):
+        return value[:, block * LANES : (block + 1) * LANES]
 
     def regroup(index, carry):
         ends = []
         for layer in range(GMAX):
             member = members_ref[(first + index) * GMAX + layer]
             holder, local = member // 2, member % 2
-            out_ref[index, layer] = held_ref[holder, local]
+            rows = held_ref[holder, local]
+            for block in range(blocks):
+                out_ref[index, KEPT * block + layer] = lanes(rows, block)
             end = held_ref[holder, 2].astype(F32)
             turned = pltpu.roll(end, TILE // 2, 0)
             ends.append(jnp.where(local == layer % 2, end, turned))
-        out_ref[index, 3] = jnp.where(upper, ends[0], ends[1]).astype(BF16)
-        out_ref[index, 4] = jnp.where(upper, ends[2], 0.0).astype(BF16)
+        pair = jnp.where(upper, ends[0], ends[1]).astype(BF16)
+        for block in range(blocks):
+            out_ref[index, KEPT * block + GMAX] = lanes(pair, block)
+        last = pltpu.roll(ends[2], TILE // 2, 0)
+        for block in range(KEPT):
+            low = lanes(last, block + KEPT) if block + KEPT < blocks else 0.0
+            value = jnp.where(upper_block, lanes(ends[2], block), low)
+            out_ref[index, KEPT * blocks + block] = value.astype(BF16)
         return carry
 
     lax.fori_loop(0, groups, regroup, 0)
@@ -191,16 +211,17 @@
 def regroup_rows(held, members):
     group_count, _, _, width = held.shape
     part = group_count // 4
+    tiles = KEPT * (width // LANES) + KEPT
     return pl.pallas_call(
         regroup_kernel,
-        out_shape=jax.ShapeDtypeStruct((group_count, OWNED, TILE, width), BF16),
+        out_shape=jax.ShapeDtypeStruct((group_count, tiles, TILE, LANES), BF16),
         grid_spec=pltpu.PrefetchScalarGridSpec(
             num_scalar_prefetch=1,
             grid=(4,),
             in_specs=[pl.BlockSpec(held.shape, lambda i, m: (0, 0, 0, 0))],
-            out_specs=pl.BlockSpec((part, OWNED, TILE, width), lambda i, m: (i, 0, 0, 0)),
-        ),
-        compiler_params=pltpu.CompilerParams(vmem_limit_bytes=32 * 1024 * 1024),
+            out_specs=pl.BlockSpec((part, tiles, TILE, LANES), lambda i, m: (i, 0, 0, 0)),
+        ),
+        compiler_params=pltpu.CompilerParams(vmem_limit_bytes=VMEM_GRANT),
         cost_estimate=pl.CostEstimate(
             flops=0, bytes_accessed=7_500_000, transcendentals=0
         ),
@@ -208,10 +229,12 @@
     )(members, held)
 
 
-def invert_kernel(rows_ref, after_ref, high_ref, low_ref, turned_ref, sys_ref):
+def invert_kernel(rows_ref, after_ref, inverse_ref, turned_ref, sys_ref):
     del after_ref
-    count, slots, _ = rows_ref.shape
+    count, blocks = rows_ref.shape[:2]
     width = count * BLK
+    kept = blocks * KEPT * TILE
+    ends = blocks * TILE
     diag = lax.broadcasted_iota(jnp.int32, (BLK, BLK), 0) == lax.broadcasted_iota(
         jnp.int32, (BLK, BLK), 1
     )
@@ -220,14 +243,18 @@
         return pl.ds(pl.multiple_of(index * BLK, BLK), BLK)
 
     def turn(i, carry):
-        turned_ref[span(i), :] = rows_ref[i].T
+        turned_ref[span(i), :kept] = rows_ref[i, :, :KEPT].reshape(kept, BLK).T
+        last = rows_ref[i, :, KEPT].reshape(ends, BLK)
+        turned_ref[span(i), kept:] = last.T
         return carry
 
     lax.fori_loop(0, count, turn, 0)
 
     def gram_block(index, carry):
         i, j = index // count, index % count
-        sys_ref[span(i), span(j)] = dot(turned_ref[span(i), :], rows_ref[j])
+        value = dot(turned_ref[span(i), :kept], rows_ref[j, :, :KEPT].reshape(kept, BLK))
+        last = rows_ref[j, :, KEPT].reshape(ends, BLK)
+        sys_ref[span(i), span(j)] = value + dot(turned_ref[span(i), kept:], last)
         return carry
 
     lax.fori_loop(0, count * count, gram_block, 0)
@@ -264,27 +291,31 @@
 
     def split(i, carry):
         high, low = halves(-sys_ref[span(i), :])
-        high_ref[span(i), :] = high
-        low_ref[span(i), :] = low
+        inverse_ref[span(i), :width] = high
+        inverse_ref[span(i), width : 2 * width] = high
+        inverse_ref[span(i), 2 * width :] = low
         return carry
 
     lax.fori_loop(0, count, split, 0)
 
 
 def invert_gram(rows, after):
-    count, slots, _ = rows.shape
+    count, blocks, _, _, _ = rows.shape
     width = count * BLK
-    square = jax.ShapeDtypeStruct((width, width), BF16)
+    slots = blocks * TILE * OWNED
     return pl.pallas_call(
         invert_kernel,
-        out_shape=(square, square, jax.ShapeDtypeStruct((width, slots), BF16)),
+        out_shape=(
+            jax.ShapeDtypeStruct((width, 3 * width), BF16),
+            jax.ShapeDtypeStruct((width, slots), BF16),
+        ),
         in_specs=[
             pl.BlockSpec(memory_space=pltpu.VMEM),
             pl.BlockSpec(memory_space=pl.ANY),
         ],
-        out_specs=[pl.BlockSpec(memory_space=pltpu.VMEM)] * 3,
+        out_specs=[pl.BlockSpec(memory_space=pltpu.VMEM)] * 2,
         scratch_shapes=[pltpu.VMEM((width, width), F32)],
-        compiler_params=pltpu.CompilerParams(vmem_limit_bytes=40 * 1024 * 1024),
+        compiler_params=pltpu.CompilerParams(vmem_limit_bytes=VMEM_GRANT),
         cost_estimate=pl.CostEstimate(
             flops=60_000_000_000, bytes_accessed=16_000_000, transcendentals=0
         ),
@@ -292,44 +323,75 @@
     )(rows, after)
 
 
-def merge_kernel(turned_ref, projected_ref, high_ref, low_ref, out_ref, first_ref, second_ref):
-    size = out_ref.shape[0]
-
-    def span(index):
-        return pl.ds(pl.multiple_of(index * BLK, BLK), BLK)
+def merge_kernel(
+    packed_hbm, turned_hbm, inverse_hbm, out_ref, packed_ref, turned_ref, inverse_ref, rows_ref, partial_ref, sems
+):
+    groups = packed_ref.shape[0]
+    size, width = out_ref.shape
+    blocks = width // LANES
+    kept = groups * KEPT * TILE
+    ends = groups * TILE
+    step = 2 * BLK
+    pairs = ((packed_hbm, packed_ref), (turned_hbm, turned_ref), (inverse_hbm, inverse_ref))
+    copies = [
+        pltpu.make_async_copy(source, target, sems.at[index])
+        for index, (source, target) in enumerate(pairs)
+    ]
+    for copy in copies:
+        copy.start()
+    copies[0].wait()
+    for block in range(blocks):
+        lanes = slice(block * LANES, (block + 1) * LANES)
+        rows = packed_ref[:, KEPT * block : KEPT * block + KEPT]
+        rows_ref[:kept, lanes] = rows.reshape(kept, LANES)
+        last = packed_ref[:, KEPT * blocks + block % KEPT].reshape(ends, LANES)
+        if block >= KEPT:
+            last = pltpu.roll(last.astype(F32), ends - TILE // 2, 0).astype(BF16)
+        rows_ref[kept:, lanes] = last
+    copies[1].wait()
+
+    def span(index, offset):
+        return pl.ds(pl.multiple_of(index * step + offset, step), step)
 
     def gather(i, carry):
-        high, low = halves(dot(turned_ref[span(i), :], projected_ref[...]))
-        first_ref[span(i), :] = high
-        second_ref[span(i), :] = low
-        return carry
-
-    lax.fori_loop(0, size // BLK, gather, 0)
+        high, low = halves(dot(turned_ref[span(i, 0), :], rows_ref[...]))
+        partial_ref[span(i, 0), :] = high
+        partial_ref[span(i, size), :] = low
+        partial_ref[span(i, 2 * size), :] = high
+        return carry
+
+    lax.fori_loop(0, size // step, gather, 0)
+    copies[2].wait()
 
     def strip(i, carry):
-        inverse = (high_ref[span(i), :], low_ref[span(i), :])
-        value = dot3(inverse, (first_ref[...], second_ref[...]))
-        out_ref[span(i), :] = value.astype(BF16)
-        return carry
-
-    lax.fori_loop(0, size // BLK, strip, 0)
-
-
-def merge_rows(turned, projected, high, low):
-    size = turned.shape[0]
-    width = projected.shape[1]
+        value = dot(inverse_ref[span(i, 0), :], partial_ref[...])
+        out_ref[span(i, 0), :] = value.astype(BF16)
+        return carry
+
+    lax.fori_loop(0, size // step, strip, 0)
+
+
+def merge_rows(packed, turned, inverse):
+    size, slots = turned.shape
+    width = (packed.shape[1] // KEPT - 1) * LANES
+    operands = (packed, turned, inverse)
     return pl.pallas_call(
         merge_kernel,
         out_shape=jax.ShapeDtypeStruct((size, width), BF16),
-        in_specs=[pl.BlockSpec(memory_space=pltpu.VMEM)] * 4,
+        in_specs=[pl.BlockSpec(memory_space=pl.ANY)] * 3,
         out_specs=pl.BlockSpec(memory_space=pltpu.VMEM),
-        scratch_shapes=[pltpu.VMEM((size, width), BF16)] * 2,
-        compiler_params=pltpu.CompilerParams(vmem_limit_bytes=40 * 1024 * 1024),
+        scratch_shapes=[pltpu.VMEM(operand.shape, BF16) for operand in operands]
+        + [
+            pltpu.VMEM((slots, width), BF16),
+            pltpu.VMEM((3 * size, width), BF16),
+            pltpu.SemaphoreType.DMA((3,)),
+        ],
+        compiler_params=pltpu.CompilerParams(vmem_limit_bytes=VMEM_GRANT),
         cost_estimate=pl.CostEstimate(
             flops=10_300_000_000, bytes_accessed=16_000_000, transcendentals=0
         ),
         name="merge_rows",
-    )(turned, projected, high, low)
+    )(*operands)
 
 
 def member_places(merge_group, group_count):
@@ -386,12 +448,12 @@
     home = exchange(projected.reshape(group_count, HELD * TILE, out_part))
     owned = lax.all_gather(at_owner, "mp", axis=0)
     regrouped = regroup_rows(home.reshape(group_count, HELD, TILE, out_part), members)
-    regrouped = regrouped.reshape(group_count, OWNED * TILE, out_part)
     arrived = exchange(regrouped)
 
-    slots = group_count * OWNED * TILE
-    high, low, turned = invert_gram(owned.reshape(parts, slots, hidden_part), regrouped)
-    merged = merge_rows(turned, arrived.reshape(slots, out_part), high, low)
+    inverse, turned = invert_gram(
+        owned.reshape(parts, group_count, OWNED, TILE, hidden_part), regrouped
+    )
+    merged = merge_rows(arrived, turned, inverse)
     return merged.reshape(1, full_width, out_part)
 
 

time: 319 us -> 308 us (0.966)
  local copies, waits for them, and re-layouts: 21.8 us -> 5.72 us
  Pallas kernels: 86.9 us -> 99.2 us
  waiting for transfers between devices: 160 us -> 153 us
    unnamed x29 -> x13, local copies, waits for them, and re-layouts: 21.5 us -> 5.4 us
    all_to_all x4, waiting for transfers between devices: 126 us -> 119 us  [exchange(): lax.all_to_all(rows, 'expert', split_axis=0, concat_axis=0, tiled=True)]
    pallas_call x1, Pallas kernels: 54.6 us -> 58.7 us  [invert_gram(): pl.pallas_call(invert_kernel, out_shape=(jax.ShapeDtypeStruct((width, 3 *...]
    pallas_call x1, Pallas kernels: 4.7 us -> 8.39 us  [project_rows(): pl.pallas_call(project_kernel, out_shape=jax.ShapeDtypeStruct((blocks, HE...]
    pallas_call x1, Pallas kernels: 2.98 us -> 6.36 us  [regroup_rows(): pl.pallas_call(regroup_kernel, out_shape=jax.ShapeDtypeStruct((group_coun...]
  transfers between devices with their start and end apart: 6 -> 6, of which waited for: 4 -> 4; matrix products, arithmetic and copies ran while one was open for 0% -> 0% of each run, Pallas kernels for 21% -> 25%
where the time goes in v3:
time: 308 us
  waiting for transfers between devices  153 us (50%)
  Pallas kernels  99.2 us (32%)
  starting transfers between devices  35.9 us (12%)
  between operations  13.5 us (4%)
  local copies, waits for them, and re-layouts  5.72 us (2%)
    all_to_all x4, waiting for transfers between devices, exchange(): lax.all_to_all(rows, 'expert', split_axis=0, concat_axis=0, tiled=True)  119 us
    pallas_call x1, Pallas kernels, invert_gram(): pl.pallas_call(invert_kernel, out_shape=(jax.ShapeDtypeStruct((width, 3 *...  58.7 us
    all_to_all x4, starting transfers between devices, exchange(): lax.all_to_all(rows, 'expert', split_axis=0, concat_axis=0, tiled=True)  35.8 us
    all_gather x1, waiting for transfers between devices, on_device(): held = lax.all_gather(at_holder, 'mp', axis=0)  33.1 us
    pallas_call x1, Pallas kernels, merge_rows(): pl.pallas_call(merge_kernel, out_shape=jax.ShapeDtypeStruct((size, width)...  17.9 us
    pallas_call x1, Pallas kernels, project_rows(): pl.pallas_call(project_kernel, out_shape=jax.ShapeDtypeStruct((blocks, HE...  8.39 us
    pallas_call x2, Pallas kernels, pack_rows(): pl.pallas_call(slot_kernel, out_shape=jax.ShapeDtypeStruct((slots, width)...  7.83 us
    pallas_call x1, Pallas kernels, regroup_rows(): pl.pallas_call(regroup_kernel, out_shape=jax.ShapeDtypeStruct((group_coun...  6.36 us
  transfers between devices with their start and end apart: 6, of which 4 were waited for; matrix products, arithmetic and copies ran while one was open for 0% of the time, Pallas kernels for 25%

profile of v3, /device:TPU:1, one launch (start us, length us, event | category | flops | bytes accessed | tf_op | source)
XLA Modules:
  0.0 307.7 jit_solution(17633571865730082998)
XLA Ops:
  6.5 0.8 copy.14
  7.3 0.1 reshape.101.routes_ref
  7.4 0.1 copy.15.bases_ref
  7.6 1.0 copy-done
  8.6 3.2 %pack_held.1 = bf16[1536,256]{1,0:T(8,128)(2,1)} custom-call(s32[1,1024]{1,0:T(1,128)S(1)} %reshape.101.routes_ref, s32[128,2]{1,0:T(8,128)S(1)} %copy.15.bases_ref, bf16[1024,256]{1,0:T(8,128)(2,1)S(1)} %bitcast.12), custom_call_target="tpu_custom_call" | custom-call | flops 3000000000 | bytes 2000000 | tf_op jit(solution)/shard_map/pack_held/pallas_call | solution.py:118
  11.8 13.0 %all-to-all-start = ((bf16[64,24,256]{2,1,0:T(8,128)(2,1)}), bf16[64,24,256]{2,1,0:T(8,128)(2,1)S(1)}, u32[]{:S(2)}, u32[]{:S(2)}) async-start(bf16[64,24,256]{2,1,0:T(8,128)(2,1)} %bitcast.1), calls=%async_computation | async-start | bytes 1572864 | tf_op jit(solution)/shard_map/all_to_all | solution.py:413
  24.8 0.0 all-gather.5.cloned.1.call-start
  24.9 0.0 copy-done.5
  24.9 0.2 convert_reduce_fusion
  25.1 0.1 copy.16.bases_ref
  25.2 0.0 copy-done.1
  25.2 4.6 %pack_owned.1 = bf16[2560,256]{1,0:T(8,128)(2,1)} custom-call(s32[1,1024]{1,0:T(1,128)S(1)} %reshape.101.routes_ref, s32[128,2]{1,0:T(8,128)S(1)} %copy.16.bases_ref, bf16[1024,256]{1,0:T(8,128)(2,1)S(1)} %bitcast.13), custom_call_target="tpu_custom_call" | custom-call | flops 3000000000 | bytes 2000000 | tf_op jit(solution)/shard_map/pack_owned/pallas_call | solution.py:118
  29.8 18.0 %all-to-all-done = bf16[64,24,256]{2,1,0:T(8,128)(2,1)S(1)} async-done(((bf16[64,24,256]{2,1,0:T(8,128)(2,1)}), bf16[64,24,256]{2,1,0:T(8,128)(2,1)S(1)}, u32[]{:S(2)}, u32[]{:S(2)}) %all-to-all-start) | async-done | bytes 786464 | tf_op jit(solution)/shard_map/all_to_all | solution.py:413
  47.8 0.9 copy-done.4
  48.7 0.0 all-gather.5.cloned.1.call-update
  48.7 6.2 %all-to-all-start.1 = ((bf16[64,40,256]{2,1,0:T(8,128)(2,1)}), bf16[64,40,256]{2,1,0:T(8,128)(2,1)S(1)}, u32[]{:S(2)}, u32[]{:S(2)}) async-start(bf16[64,40,256]{2,1,0:T(8,128)(2,1)} %bitcast.4), calls=%async_computation.1 | async-start | bytes 2621440 | tf_op jit(solution)/shard_map/all_to_all | solution.py:413
  54.9 33.1 %all-gather.5.cloned.1.call-done = bf16[256,24,256]{2,1,0:T(8,128)(2,1)} async-done(((bf16[64,24,256]{2,1,0:T(8,128)(2,1)}), bf16[256,24,256]{2,1,0:T(8,128)(2,1)}) %all-gather.5.cloned.1.call-update) | async-done | bytes 3145744 | tf_op jit(solution)/shard_map/all_gather | solution.py:441
  88.0 8.4 %project_rows.1 = bf16[64,3,8,896]{3,2,1,0:T(8,128)(2,1)} custom-call(bf16[4,64,3,8,256]{4,3,2,1,0:T(8,128)(2,1)} %bitcast.17, bf16[2,1024,896]{2,1,0:T(8,128)(2,1)} %weights_ref.1), custom_call_target="tpu_custom_call" | custom-call | flops 4000000000 | bytes 10000000 | tf_op jit(solution)/shard_map/project_rows/pallas_call | solution.py:159
  96.4 0.0 all-to-all-done.1
  96.4 1.1 copy-done.3
  97.5 10.7 %all-to-all-start.2 = ((bf16[64,24,896]{2,1,0:T(8,128)(2,1)}), bf16[64,24,896]{2,1,0:T(8,128)(2,1)S(1)}, u32[]{:S(2)}, u32[]{:S(2)}) async-start(bf16[64,24,896]{2,1,0:T(8,128)(2,1)} %bitcast.15), calls=%async_computation.2 | async-start | bytes 5505024 | tf_op jit(solution)/shard_map/all_to_all | solution.py:413
  108.1 0.0 all-gather.7.cloned.1.call-start
  108.2 0.7 all-gather.7.cloned.1.call-update
  108.9 0.6 select_reduce_fusion.members_ref
  109.5 63.7 %all-to-all-done.2 = bf16[64,24,896]{2,1,0:T(8,128)(2,1)S(1)} async-done(((bf16[64,24,896]{2,1,0:T(8,128)(2,1)}), bf16[64,24,896]{2,1,0:T(8,128)(2,1)S(1)}, u32[]{:S(2)}, u32[]{:S(2)}) %all-to-all-start.2) | async-done | bytes 2752544 | tf_op jit(solution)/shard_map/all_to_all | solution.py:413
  173.2 1.6 copy-done.2
  174.8 6.4 %regroup_rows.1.after_ref = bf16[64,32,8,128]{3,2,1,0:T(8,128)(2,1)} custom-call(s32[192]{0:T(256)} %select_reduce_fusion.members_ref, bf16[64,3,8,896]{3,2,1,0:T(8,128)(2,1)} %bitcast.14), custom_call_target="tpu_custom_call" | custom-call | bytes 7500000 | tf_op jit(solution)/shard_map/regroup_rows/pallas_call | solution.py:215
  181.2 5.9 %all-to-all-start.3 = ((bf16[64,32,8,128]{3,2,1,0:T(8,128)(2,1)}), bf16[64,32,8,128]{3,2,1,0:T(8,128)(2,1)}, u32[]{:S(2)}, u32[]{:S(2)}) async-start(bf16[64,32,8,128]{3,2,1,0:T(8,128)(2,1)} %regroup_rows.1.after_ref), calls=%async_computation.3 | async-start | bytes 8388608 | tf_op jit(solution)/shard_map/all_to_all | solution.py:413
  187.1 0.0 all-gather.7.cloned.1.call-done
  187.1 58.7 %invert_gram.1 = (bf16[1024,3072]{1,0:T(8,128)(2,1)}, bf16[1024,2560]{1,0:T(8,128)(2,1)}) custom-call(bf16[4,64,5,8,256]{4,3,2,1,0:T(8,128)(2,1)} %bitcast.16, bf16[64,32,8,128]{3,2,1,0:T(8,128)(2,1)} %regroup_rows.1.after_ref), custom_call_target="tpu_custom_call" | custom-call | flops 60000002048 | bytes 16000000 | tf_op jit(solution)/shard_map/invert_gram/pallas_call | solution.py:306
  245.8 37.1 %all-to-all-done.3.packed_hbm = bf16[64,32,8,128]{3,2,1,0:T(8,128)(2,1)} async-done(((bf16[64,32,8,128]{3,2,1,0:T(8,128)(2,1)}), bf16[64,32,8,128]{3,2,1,0:T(8,128)(2,1)}, u32[]{:S(2)}, u32[]{:S(2)}) %all-to-all-start.3) | async-done | bytes 4194336 | tf_op jit(solution)/shard_map/all_to_all | solution.py:413
  283.0 17.9 %merge_rows.1 = bf16[1024,896]{1,0:T(8,128)(2,1)} custom-call(bf16[64,32,8,128]{3,2,1,0:T(8,128)(2,1)} %all-to-all-done.3.packed_hbm, bf16[1024,2560]{1,0:T(8,128)(2,1)} %get-tuple-element.15.turned_hbm, bf16[1024,3072]{1,0:T(8,128)(2,1)} %get-tuple-element.16.inverse_hbm), custom_call_target="tpu_custom_call" | custom-call | flops 10300000256 | bytes 16000000 | tf_op jit(solution)/shard_map/merge_rows/pallas_call | solution.py:378
  (10 shorter events, 0.0 us)
Async XLA Ops:
  7.6 1.0 copy-start
  8.6 16.3 %copy-start.5 = (s32[128]{0:T(128)S(1)}, s32[128]{0:T(128)}, u32[]{:S(2)}) copy-start(s32[128]{0:T(128)} %param.7) | copy-start | bytes 1540
  8.6 16.6 %copy-start.1 = (bf16[128,8,256]{2,1,0:T(8,128)(2,1)S(1)}, bf16[128,8,256]{2,1,0:T(8,128)(2,1)}, u32[]{:S(2)}) copy-start(bf16[128,8,256]{2,1,0:T(8,128)(2,1)} %param.5) | copy-start | bytes 1572868
  11.8 36.0 %all-to-all-start = ((bf16[64,24,256]{2,1,0:T(8,128)(2,1)}), bf16[64,24,256]{2,1,0:T(8,128)(2,1)S(1)}, u32[]{:S(2)}, u32[]{:S(2)}) async-start(bf16[64,24,256]{2,1,0:T(8,128)(2,1)} %bitcast.1), calls=%async_computation | async-start | bytes 1572864 | tf_op jit(solution)/shard_map/all_to_all | solution.py:413
  24.8 63.2 %all-gather.5.cloned.1.call-start = ((), (), s32[]{:S(2)}) async-start(), calls=%async_computation.4 | async-start | bytes 3932160 | tf_op jit(solution)/shard_map/all_gather | solution.py:441
  47.8 0.9 copy-start.4
  48.7 47.7 %all-to-all-start.1 = ((bf16[64,40,256]{2,1,0:T(8,128)(2,1)}), bf16[64,40,256]{2,1,0:T(8,128)(2,1)S(1)}, u32[]{:S(2)}, u32[]{:S(2)}) async-start(bf16[64,40,256]{2,1,0:T(8,128)(2,1)} %bitcast.4), calls=%async_computation.1 | async-start | bytes 2621440 | tf_op jit(solution)/shard_map/all_to_all | solution.py:413
  96.4 1.1 copy-start.3
  97.5 75.7 %all-to-all-start.2 = ((bf16[64,24,896]{2,1,0:T(8,128)(2,1)}), bf16[64,24,896]{2,1,0:T(8,128)(2,1)S(1)}, u32[]{:S(2)}, u32[]{:S(2)}) async-start(bf16[64,24,896]{2,1,0:T(8,128)(2,1)} %bitcast.15), calls=%async_computation.2 | async-start | bytes 5505024 | tf_op jit(solution)/shard_map/all_to_all | solution.py:413
  108.1 79.0 %all-gather.7.cloned.1.call-start = ((), (), s32[]{:S(2)}) async-start(), calls=%async_computation.5 | async-start | bytes 6553600 | tf_op jit(solution)/shard_map/all_gather | solution.py:449
  173.2 1.6 copy-start.2
  181.2 101.8 %all-to-all-start.3 = ((bf16[64,32,8,128]{3,2,1,0:T(8,128)(2,1)}), bf16[64,32,8,128]{3,2,1,0:T(8,128)(2,1)}, u32[]{:S(2)}, u32[]{:S(2)}) async-start(bf16[64,32,8,128]{3,2,1,0:T(8,128)(2,1)} %regroup_rows.1.after_ref), calls=%async_computation.3 | async-start | bytes 8388608 | tf_op jit(solution)/shard_map/all_to_all | solution.py:413
Sparse Core Ops, SparseCore 0:
  48.8 39.1 all-gather.4
  110.8 59.3 all-gather.6

commit v4 on v3

--- a/solution.py
+++ b/solution.py
@@ -86,6 +86,8 @@
 OWNED = 5
 KEPT = 4
 LANES = 128
+UNROLL = 4
+PROJECT_STEP = 32
 VMEM_GRANT = 58 * 1024 * 1024
 
 
@@ -155,7 +157,7 @@
 def project_rows(rows, weights):
     parts, blocks, _, _, hidden_part = rows.shape
     width = weights.shape[2]
-    step = 16
+    step = PROJECT_STEP
     return pl.pallas_call(
         project_kernel,
         out_shape=jax.ShapeDtypeStruct((blocks, HELD, TILE, width), BF16),
@@ -173,9 +175,8 @@
     )(rows, weights)
 
 
-def regroup_kernel(members_ref, held_ref, out_ref):
-    groups = out_ref.shape[0]
-    first = pl.program_id(0) * groups
+def regroup_kernel(members_ref, held_ref, out_hbm, out_ref, sems):
+    parts, groups = out_ref.shape[:2]
     width = held_ref.shape[3]
     blocks = width // LANES
     upper = lax.broadcasted_iota(jnp.int32, (TILE, width), 0) < TILE // 2
@@ -184,44 +185,62 @@
     def lanes(value, block):
         return value[:, block * LANES : (block + 1) * LANES]
 
-    def regroup(index, carry):
+    def regroup(part, index):
         ends = []
         for layer in range(GMAX):
-            member = members_ref[(first + index) * GMAX + layer]
-            holder, local = member // 2, member % 2
+            member = members_ref[(part * groups + index) * GMAX + layer]
+            holder, local = member >> 1, member & 1
             rows = held_ref[holder, local]
             for block in range(blocks):
-                out_ref[index, KEPT * block + layer] = lanes(rows, block)
+                out_ref[part, index, KEPT * block + layer] = lanes(rows, block)
             end = held_ref[holder, 2].astype(F32)
             turned = pltpu.roll(end, TILE // 2, 0)
             ends.append(jnp.where(local == layer % 2, end, turned))
         pair = jnp.where(upper, ends[0], ends[1]).astype(BF16)
         for block in range(blocks):
-            out_ref[index, KEPT * block + GMAX] = lanes(pair, block)
+            out_ref[part, index, KEPT * block + GMAX] = lanes(pair, block)
         last = pltpu.roll(ends[2], TILE // 2, 0)
         for block in range(KEPT):
             low = lanes(last, block + KEPT) if block + KEPT < blocks else 0.0
             value = jnp.where(upper_block, lanes(ends[2], block), low)
-            out_ref[index, KEPT * blocks + block] = value.astype(BF16)
-        return carry
-
-    lax.fori_loop(0, groups, regroup, 0)
+            out_ref[part, index, KEPT * blocks + block] = value.astype(BF16)
+
+    copies = []
+    for part in range(parts):
+
+        def several(index, carry, part=part):
+            for k in range(UNROLL):
+                regroup(part, index * UNROLL + k)
+            return carry
+
+        lax.fori_loop(0, groups // UNROLL, several, 0)
+        copies.append(
+            pltpu.make_async_copy(
+                out_ref.at[part], out_hbm.at[pl.ds(part * groups, groups)], sems.at[part]
+            )
+        )
+        copies[-1].start()
+    for copy in copies:
+        copy.wait()
 
 
 def regroup_rows(held, members):
     group_count, _, _, width = held.shape
-    part = group_count // 4
+    parts = 4
     tiles = KEPT * (width // LANES) + KEPT
     return pl.pallas_call(
         regroup_kernel,
         out_shape=jax.ShapeDtypeStruct((group_count, tiles, TILE, LANES), BF16),
-        grid_spec=pltpu.PrefetchScalarGridSpec(
-            num_scalar_prefetch=1,
-            grid=(4,),
-            in_specs=[pl.BlockSpec(held.shape, lambda i, m: (0, 0, 0, 0))],
-            out_specs=pl.BlockSpec((part, tiles, TILE, LANES), lambda i, m: (i, 0, 0, 0)),
-        ),
-        compiler_params=pltpu.CompilerParams(vmem_limit_bytes=VMEM_GRANT),
+        in_specs=[
+            pl.BlockSpec(memory_space=pltpu.SMEM),
+            pl.BlockSpec(memory_space=pltpu.VMEM),
+        ],
+        out_specs=pl.BlockSpec(memory_space=pltpu.HBM),
+        scratch_shapes=[
+            pltpu.VMEM((parts, group_count // parts, tiles, TILE, LANES), BF16),
+            pltpu.SemaphoreType.DMA((parts,)),
+        ],
+        compiler_params=pltpu.CompilerParams(vmem_limit_bytes=16 * 1024 * 1024),
         cost_estimate=pl.CostEstimate(
             flops=0, bytes_accessed=7_500_000, transcendentals=0
         ),
@@ -229,7 +248,7 @@
     )(members, held)
 
 
-def invert_kernel(rows_ref, after_ref, inverse_ref, turned_ref, sys_ref):
+def invert_kernel(rows_ref, after_ref, maps_ref, turned_ref, sys_ref):
     del after_ref
     count, blocks = rows_ref.shape[:2]
     width = count * BLK
@@ -289,14 +308,19 @@
 
     lax.fori_loop(0, count, sweep, 0)
 
-    def split(i, carry):
-        high, low = halves(-sys_ref[span(i), :])
-        inverse_ref[span(i), :width] = high
-        inverse_ref[span(i), width : 2 * width] = high
-        inverse_ref[span(i), 2 * width :] = low
+    def map_block(index, carry):
+        i, j = index // strips, index % strips
+        here = pl.ds(pl.multiple_of(j * strip, strip), strip)
+        both = jnp.concatenate(halves(-sys_ref[span(i), :]), axis=0)
+        value = dot(both, turned_ref[:, here])
+        high, low = halves(value[:BLK] + value[BLK:])
+        maps_ref[span(2 * i), here] = high
+        maps_ref[span(2 * i + 1), here] = low
         return carry
 
-    lax.fori_loop(0, count, split, 0)
+    strip = 2 * BLK
+    strips = (kept + ends) // strip
+    lax.fori_loop(0, count * strips, map_block, 0)
 
 
 def invert_gram(rows, after):
@@ -305,16 +329,13 @@
     slots = blocks * TILE * OWNED
     return pl.pallas_call(
         invert_kernel,
-        out_shape=(
-            jax.ShapeDtypeStruct((width, 3 * width), BF16),
-            jax.ShapeDtypeStruct((width, slots), BF16),
-        ),
+        out_shape=jax.ShapeDtypeStruct((2 * width, slots), BF16),
         in_specs=[
             pl.BlockSpec(memory_space=pltpu.VMEM),
             pl.BlockSpec(memory_space=pl.ANY),
         ],
-        out_specs=[pl.BlockSpec(memory_space=pltpu.VMEM)] * 2,
-        scratch_shapes=[pltpu.VMEM((width, width), F32)],
+        out_specs=pl.BlockSpec(memory_space=pltpu.VMEM),
+        scratch_shapes=[pltpu.VMEM((width, slots), BF16), pltpu.VMEM((width, width), F32)],
         compiler_params=pltpu.CompilerParams(vmem_limit_bytes=VMEM_GRANT),
         cost_estimate=pl.CostEstimate(
             flops=60_000_000_000, bytes_accessed=16_000_000, transcendentals=0
@@ -323,23 +344,22 @@
     )(rows, after)
 
 
-def merge_kernel(
-    packed_hbm, turned_hbm, inverse_hbm, out_ref, packed_ref, turned_ref, inverse_ref, rows_ref, partial_ref, sems
-):
+def merge_kernel(packed_hbm, maps_hbm, out_ref, packed_ref, maps_ref, rows_ref, sems):
     groups = packed_ref.shape[0]
     size, width = out_ref.shape
     blocks = width // LANES
     kept = groups * KEPT * TILE
     ends = groups * TILE
-    step = 2 * BLK
-    pairs = ((packed_hbm, packed_ref), (turned_hbm, turned_ref), (inverse_hbm, inverse_ref))
-    copies = [
-        pltpu.make_async_copy(source, target, sems.at[index])
-        for index, (source, target) in enumerate(pairs)
-    ]
-    for copy in copies:
-        copy.start()
-    copies[0].wait()
+    first = pltpu.make_async_copy(packed_hbm, packed_ref, sems.at[0])
+    first.start()
+    copies = []
+    for index in range(size // BLK):
+        here = slice(2 * index * BLK, 2 * (index + 1) * BLK)
+        copies.append(
+            pltpu.make_async_copy(maps_hbm.at[here], maps_ref.at[here], sems.at[index + 1])
+        )
+        copies[-1].start()
+    first.wait()
     for block in range(blocks):
         lanes = slice(block * LANES, (block + 1) * LANES)
         rows = packed_ref[:, KEPT * block : KEPT * block + KEPT]
@@ -348,50 +368,33 @@
         if block >= KEPT:
             last = pltpu.roll(last.astype(F32), ends - TILE // 2, 0).astype(BF16)
         rows_ref[kept:, lanes] = last
-    copies[1].wait()
-
-    def span(index, offset):
-        return pl.ds(pl.multiple_of(index * step + offset, step), step)
-
-    def gather(i, carry):
-        high, low = halves(dot(turned_ref[span(i, 0), :], rows_ref[...]))
-        partial_ref[span(i, 0), :] = high
-        partial_ref[span(i, size), :] = low
-        partial_ref[span(i, 2 * size), :] = high
-        return carry
-
-    lax.fori_loop(0, size // step, gather, 0)
-    copies[2].wait()
-
-    def strip(i, carry):
-        value = dot(inverse_ref[span(i, 0), :], partial_ref[...])
-        out_ref[span(i, 0), :] = value.astype(BF16)
-        return carry
-
-    lax.fori_loop(0, size // step, strip, 0)
-
-
-def merge_rows(packed, turned, inverse):
-    size, slots = turned.shape
+    for index, copy in enumerate(copies):
+        copy.wait()
+        value = dot(maps_ref[2 * index * BLK : 2 * (index + 1) * BLK], rows_ref[...])
+        here = slice(index * BLK, (index + 1) * BLK)
+        out_ref[here] = (value[:BLK] + value[BLK:]).astype(BF16)
+
+
+def merge_rows(packed, maps):
+    size, slots = maps.shape
     width = (packed.shape[1] // KEPT - 1) * LANES
-    operands = (packed, turned, inverse)
     return pl.pallas_call(
         merge_kernel,
-        out_shape=jax.ShapeDtypeStruct((size, width), BF16),
-        in_specs=[pl.BlockSpec(memory_space=pl.ANY)] * 3,
+        out_shape=jax.ShapeDtypeStruct((size // 2, width), BF16),
+        in_specs=[pl.BlockSpec(memory_space=pl.ANY)] * 2,
         out_specs=pl.BlockSpec(memory_space=pltpu.VMEM),
-        scratch_shapes=[pltpu.VMEM(operand.shape, BF16) for operand in operands]
-        + [
+        scratch_shapes=[
+            pltpu.VMEM(packed.shape, BF16),
+            pltpu.VMEM(maps.shape, BF16),
             pltpu.VMEM((slots, width), BF16),
-            pltpu.VMEM((3 * size, width), BF16),
-            pltpu.SemaphoreType.DMA((3,)),
+            pltpu.SemaphoreType.DMA((1 + size // (2 * BLK),)),
         ],
         compiler_params=pltpu.CompilerParams(vmem_limit_bytes=VMEM_GRANT),
         cost_estimate=pl.CostEstimate(
-            flops=10_300_000_000, bytes_accessed=16_000_000, transcendentals=0
+            flops=9_400_000_000, bytes_accessed=16_000_000, transcendentals=0
         ),
         name="merge_rows",
-    )(*operands)
+    )(packed, maps)
 
 
 def member_places(merge_group, group_count):
@@ -450,10 +453,10 @@
     regrouped = regroup_rows(home.reshape(group_count, HELD, TILE, out_part), members)
     arrived = exchange(regrouped)
 
-    inverse, turned = invert_gram(
+    maps = invert_gram(
         owned.reshape(parts, group_count, OWNED, TILE, hidden_part), regrouped
     )
-    merged = merge_rows(arrived, turned, inverse)
+    merged = merge_rows(arrived, maps)
     return merged.reshape(1, full_width, out_part)
 
 

time: 308 us -> 302 us (0.981)
  waiting for transfers between devices: 153 us -> 139 us
  Pallas kernels: 99.2 us -> 107 us
    all_to_all x4, waiting for transfers between devices: 119 us -> 105 us  [exchange(): lax.all_to_all(rows, 'expert', split_axis=0, concat_axis=0, tiled=True)]
    pallas_call x2, Pallas kernels: 76.6 us -> 88.6 us  [the longest x1 72.9 us: invert_gram(): pl.pallas_call(invert_kernel, out_shape=jax.ShapeDtypeStruct((2 * width,...]
    pallas_call x1, Pallas kernels: 6.36 us -> 2.1 us  [regroup_rows(): pl.pallas_call(regroup_kernel, out_shape=jax.ShapeDtypeStruct((group_coun...]
  transfers between devices with their start and end apart: 6 -> 6, of which waited for: 4 -> 4; matrix products, arithmetic and copies ran while one was open for 0% -> 0% of each run, Pallas kernels for 25% -> 29%
where the time goes in v4:
time: 302 us
  waiting for transfers between devices  139 us (46%)
  Pallas kernels  107 us (35%)
  starting transfers between devices  35.9 us (12%)
  between operations  13.5 us (4%)
  local copies, waits for them, and re-layouts  6.1 us (2%)
    all_to_all x4, waiting for transfers between devices, exchange(): lax.all_to_all(rows, 'expert', split_axis=0, concat_axis=0, tiled=True)  105 us
    pallas_call x1, Pallas kernels, invert_gram(): pl.pallas_call(invert_kernel, out_shape=jax.ShapeDtypeStruct((2 * width,...  72.9 us
    all_to_all x4, starting transfers between devices, exchange(): lax.all_to_all(rows, 'expert', split_axis=0, concat_axis=0, tiled=True)  35.8 us
    all_gather x1, waiting for transfers between devices, on_device(): held = lax.all_gather(at_holder, 'mp', axis=0)  33.1 us
    pallas_call x1, Pallas kernels, merge_rows(): pl.pallas_call(merge_kernel, out_shape=jax.ShapeDtypeStruct((size // 2, w...  15.7 us
    pallas_call x1, Pallas kernels, project_rows(): pl.pallas_call(project_kernel, out_shape=jax.ShapeDtypeStruct((blocks, HE...  8.33 us
    pallas_call x2, Pallas kernels, pack_rows(): pl.pallas_call(slot_kernel, out_shape=jax.ShapeDtypeStruct((slots, width)...  7.82 us
  transfers between devices with their start and end apart: 6, of which 4 were waited for; matrix products, arithmetic and copies ran while one was open for 0% of the time, Pallas kernels for 29%

profile of v4, /device:TPU:1, one launch (start us, length us, event | category | flops | bytes accessed | tf_op | source)
XLA Modules:
  0.0 301.7 jit_solution(15637200872389022132)
XLA Ops:
  6.5 0.8 copy.14
  7.3 0.1 reshape.101.routes_ref
  7.4 0.1 copy.15.bases_ref
  7.6 1.0 copy-done.1
  8.6 3.2 %pack_held.1 = bf16[1536,256]{1,0:T(8,128)(2,1)} custom-call(s32[1,1024]{1,0:T(1,128)S(1)} %reshape.101.routes_ref, s32[128,2]{1,0:T(8,128)S(1)} %copy.15.bases_ref, bf16[1024,256]{1,0:T(8,128)(2,1)S(1)} %bitcast.13), custom_call_target="tpu_custom_call" | custom-call | flops 3000000000 | bytes 2000000 | tf_op jit(solution)/shard_map/pack_held/pallas_call | solution.py:120
  11.8 13.0 %all-to-all-start = ((bf16[64,24,256]{2,1,0:T(8,128)(2,1)}), bf16[64,24,256]{2,1,0:T(8,128)(2,1)S(1)}, u32[]{:S(2)}, u32[]{:S(2)}) async-start(bf16[64,24,256]{2,1,0:T(8,128)(2,1)} %bitcast.1), calls=%async_computation | async-start | bytes 1572864 | tf_op jit(solution)/shard_map/all_to_all | solution.py:416
  24.8 0.0 all-gather.5.cloned.1.call-start
  24.9 0.0 copy-done.5
  24.9 0.2 convert_reduce_fusion
  25.1 0.1 copy.16.bases_ref
  25.2 0.0 copy-done.2
  25.2 4.6 %pack_owned.1 = bf16[2560,256]{1,0:T(8,128)(2,1)} custom-call(s32[1,1024]{1,0:T(1,128)S(1)} %reshape.101.routes_ref, s32[128,2]{1,0:T(8,128)S(1)} %copy.16.bases_ref, bf16[1024,256]{1,0:T(8,128)(2,1)S(1)} %bitcast.14), custom_call_target="tpu_custom_call" | custom-call | flops 3000000000 | bytes 2000000 | tf_op jit(solution)/shard_map/pack_owned/pallas_call | solution.py:120
  29.8 18.0 %all-to-all-done = bf16[64,24,256]{2,1,0:T(8,128)(2,1)S(1)} async-done(((bf16[64,24,256]{2,1,0:T(8,128)(2,1)}), bf16[64,24,256]{2,1,0:T(8,128)(2,1)S(1)}, u32[]{:S(2)}, u32[]{:S(2)}) %all-to-all-start) | async-done | bytes 786464 | tf_op jit(solution)/shard_map/all_to_all | solution.py:416
  47.8 0.9 copy-done.4
  48.7 0.0 all-gather.5.cloned.1.call-update
  48.7 6.2 %all-to-all-start.1 = ((bf16[64,40,256]{2,1,0:T(8,128)(2,1)}), bf16[64,40,256]{2,1,0:T(8,128)(2,1)S(1)}, u32[]{:S(2)}, u32[]{:S(2)}) async-start(bf16[64,40,256]{2,1,0:T(8,128)(2,1)} %bitcast.4), calls=%async_computation.1 | async-start | bytes 2621440 | tf_op jit(solution)/shard_map/all_to_all | solution.py:416
  54.9 33.1 %all-gather.5.cloned.1.call-done = bf16[256,24,256]{2,1,0:T(8,128)(2,1)} async-done(((bf16[64,24,256]{2,1,0:T(8,128)(2,1)}), bf16[256,24,256]{2,1,0:T(8,128)(2,1)}) %all-gather.5.cloned.1.call-update) | async-done | bytes 3145744 | tf_op jit(solution)/shard_map/all_gather | solution.py:444
  88.0 8.3 %project_rows.1 = bf16[64,3,8,896]{3,2,1,0:T(8,128)(2,1)} custom-call(bf16[4,64,3,8,256]{4,3,2,1,0:T(8,128)(2,1)} %bitcast.17, bf16[2,1024,896]{2,1,0:T(8,128)(2,1)} %weights_ref.1), custom_call_target="tpu_custom_call" | custom-call | flops 4000000000 | bytes 10000000 | tf_op jit(solution)/shard_map/project_rows/pallas_call | solution.py:161
  96.4 0.0 all-to-all-done.1
  96.4 1.1 copy-done.3
  97.4 10.7 %all-to-all-start.2 = ((bf16[64,24,896]{2,1,0:T(8,128)(2,1)}), bf16[64,24,896]{2,1,0:T(8,128)(2,1)S(1)}, u32[]{:S(2)}, u32[]{:S(2)}) async-start(bf16[64,24,896]{2,1,0:T(8,128)(2,1)} %bitcast.15), calls=%async_computation.2 | async-start | bytes 5505024 | tf_op jit(solution)/shard_map/all_to_all | solution.py:416
  108.1 0.0 all-gather.7.cloned.1.call-start
  108.1 0.7 all-gather.7.cloned.1.call-update
  108.8 0.1 select_reduce_fusion.members_ref
  109.0 64.2 %all-to-all-done.2 = bf16[64,24,896]{2,1,0:T(8,128)(2,1)S(1)} async-done(((bf16[64,24,896]{2,1,0:T(8,128)(2,1)}), bf16[64,24,896]{2,1,0:T(8,128)(2,1)S(1)}, u32[]{:S(2)}, u32[]{:S(2)}) %all-to-all-start.2) | async-done | bytes 2752544 | tf_op jit(solution)/shard_map/all_to_all | solution.py:416
  173.2 2.1 regroup_rows.1.after_ref
  175.3 2.0 copy-done
  177.3 5.9 %all-to-all-start.3 = ((bf16[64,32,8,128]{3,2,1,0:T(8,128)(2,1)}), bf16[64,32,8,128]{3,2,1,0:T(8,128)(2,1)}, u32[]{:S(2)}, u32[]{:S(2)}) async-start(bf16[64,32,8,128]{3,2,1,0:T(8,128)(2,1)} %copy-done), calls=%async_computation.3 | async-start | bytes 8388608 | tf_op jit(solution)/shard_map/all_to_all | solution.py:416
  183.2 0.0 all-gather.7.cloned.1.call-done
  183.2 72.9 %invert_gram.1.maps_hbm = bf16[2048,2560]{1,0:T(8,128)(2,1)} custom-call(bf16[4,64,5,8,256]{4,3,2,1,0:T(8,128)(2,1)} %bitcast.16, bf16[64,32,8,128]{3,2,1,0:T(8,128)(2,1)} %copy-done), custom_call_target="tpu_custom_call" | custom-call | flops 60000002048 | bytes 16000000 | tf_op jit(solution)/shard_map/invert_gram/pallas_call | solution.py:330
  256.1 23.0 %all-to-all-done.3.packed_hbm = bf16[64,32,8,128]{3,2,1,0:T(8,128)(2,1)} async-done(((bf16[64,32,8,128]{3,2,1,0:T(8,128)(2,1)}), bf16[64,32,8,128]{3,2,1,0:T(8,128)(2,1)}, u32[]{:S(2)}, u32[]{:S(2)}) %all-to-all-start.3) | async-done | bytes 4194336 | tf_op jit(solution)/shard_map/all_to_all | solution.py:416
  279.1 15.7 %merge_rows.1 = bf16[1024,896]{1,0:T(8,128)(2,1)} custom-call(bf16[64,32,8,128]{3,2,1,0:T(8,128)(2,1)} %all-to-all-done.3.packed_hbm, bf16[2048,2560]{1,0:T(8,128)(2,1)} %invert_gram.1.maps_hbm), custom_call_target="tpu_custom_call" | custom-call | flops 9400000512 | bytes 16000000 | tf_op jit(solution)/shard_map/merge_rows/pallas_call | solution.py:381
  (10 shorter events, 0.0 us)
Async XLA Ops:
  7.6 1.0 copy-start.1
  8.6 16.3 %copy-start.5 = (s32[128]{0:T(128)S(1)}, s32[128]{0:T(128)}, u32[]{:S(2)}) copy-start(s32[128]{0:T(128)} %param.7) | copy-start | bytes 1540
  8.6 16.6 %copy-start.2 = (bf16[128,8,256]{2,1,0:T(8,128)(2,1)S(1)}, bf16[128,8,256]{2,1,0:T(8,128)(2,1)}, u32[]{:S(2)}) copy-start(bf16[128,8,256]{2,1,0:T(8,128)(2,1)} %param.5) | copy-start | bytes 1572868
  11.8 36.0 %all-to-all-start = ((bf16[64,24,256]{2,1,0:T(8,128)(2,1)}), bf16[64,24,256]{2,1,0:T(8,128)(2,1)S(1)}, u32[]{:S(2)}, u32[]{:S(2)}) async-start(bf16[64,24,256]{2,1,0:T(8,128)(2,1)} %bitcast.1), calls=%async_computation | async-start | bytes 1572864 | tf_op jit(solution)/shard_map/all_to_all | solution.py:416
  24.8 63.2 %all-gather.5.cloned.1.call-start = ((), (), s32[]{:S(2)}) async-start(), calls=%async_computation.4 | async-start | bytes 3932160 | tf_op jit(solution)/shard_map/all_gather | solution.py:444
  47.8 0.9 copy-start.4
  48.7 47.6 %all-to-all-start.1 = ((bf16[64,40,256]{2,1,0:T(8,128)(2,1)}), bf16[64,40,256]{2,1,0:T(8,128)(2,1)S(1)}, u32[]{:S(2)}, u32[]{:S(2)}) async-start(bf16[64,40,256]{2,1,0:T(8,128)(2,1)} %bitcast.4), calls=%async_computation.1 | async-start | bytes 2621440 | tf_op jit(solution)/shard_map/all_to_all | solution.py:416
  96.4 1.1 copy-start.3
  97.4 75.7 %all-to-all-start.2 = ((bf16[64,24,896]{2,1,0:T(8,128)(2,1)}), bf16[64,24,896]{2,1,0:T(8,128)(2,1)S(1)}, u32[]{:S(2)}, u32[]{:S(2)}) async-start(bf16[64,24,896]{2,1,0:T(8,128)(2,1)} %bitcast.15), calls=%async_computation.2 | async-start | bytes 5505024 | tf_op jit(solution)/shard_map/all_to_all | solution.py:416
  108.1 75.1 %all-gather.7.cloned.1.call-start = ((), (), s32[]{:S(2)}) async-start(), calls=%async_computation.5 | async-start | bytes 6553600 | tf_op jit(solution)/shard_map/all_gather | solution.py:452
  175.3 2.0 copy-start
  177.3 101.8 %all-to-all-start.3 = ((bf16[64,32,8,128]{3,2,1,0:T(8,128)(2,1)}), bf16[64,32,8,128]{3,2,1,0:T(8,128)(2,1)}, u32[]{:S(2)}, u32[]{:S(2)}) async-start(bf16[64,32,8,128]{3,2,1,0:T(8,128)(2,1)} %copy-done), calls=%async_computation.3 | async-start | bytes 8388608 | tf_op jit(solution)/shard_map/all_to_all | solution.py:416
Sparse Core Ops, SparseCore 0:
  48.8 39.1 all-gather.4
  110.7 59.3 all-gather.6

commit v5 on v4

--- a/solution.py
+++ b/solution.py
@@ -87,11 +87,13 @@
 KEPT = 4
 LANES = 128
 UNROLL = 4
-PROJECT_STEP = 32
+PROJECT_PARTS = 2
 VMEM_GRANT = 58 * 1024 * 1024
 
 
-def slot_kernel(routes_ref, bases_ref, rows_ref, out_ref, slot_ref):
+def slot_kernel(routes_ref, bases_ref, rows_hbm, out_ref, slot_ref, rows_ref, sem):
+    copy = pltpu.make_async_copy(rows_hbm, rows_ref, sem)
+    copy.start()
     experts = bases_ref.shape[0]
     count = routes_ref.shape[1]
     hit = lax.broadcasted_iota(jnp.int32, (experts, count), 0) == routes_ref[...]
@@ -104,6 +106,7 @@
     place = before + jnp.where(before < TILE, bases[:, 0:1], bases[:, 1:2])
     slot = jnp.sum(jnp.where(hit, place, 0.0), axis=0, keepdims=True)
     slot_ref[...] = slot.astype(jnp.int32)
+    copy.wait()
 
     def fill(index, carry):
         here = pl.multiple_of(index * BLK, BLK)
@@ -120,10 +123,15 @@
     return pl.pallas_call(
         slot_kernel,
         out_shape=jax.ShapeDtypeStruct((slots, width), BF16),
-        in_specs=[pl.BlockSpec(memory_space=pltpu.VMEM)] * 3,
+        in_specs=[pl.BlockSpec(memory_space=pltpu.VMEM)] * 2
+        + [pl.BlockSpec(memory_space=pl.ANY)],
         out_specs=pl.BlockSpec(memory_space=pltpu.VMEM),
-        scratch_shapes=[pltpu.VMEM((1, count), jnp.int32)],
-        compiler_params=pltpu.CompilerParams(vmem_limit_bytes=32 * 1024 * 1024),
+        scratch_shapes=[
+            pltpu.VMEM((1, count), jnp.int32),
+            pltpu.VMEM(rows.shape, BF16),
+            pltpu.SemaphoreType.DMA,
+        ],
+        compiler_params=pltpu.CompilerParams(vmem_limit_bytes=VMEM_GRANT),
         cost_estimate=pl.CostEstimate(
             flops=3_000_000_000, bytes_accessed=2_000_000, transcendentals=0
         ),
@@ -131,42 +139,90 @@
     )(routes, bases, rows)
 
 
-def project_kernel(rows_ref, weights_ref, out_ref):
+def project_kernel(
+    rows_hbm, weights_hbm, out_hbm, rows_ref, weights_ref, out_ref, mixed_ref, row_sems, weight_sems, out_sems
+):
     parts, blocks = rows_ref.shape[:2]
     width = out_ref.shape[3]
-    slots = blocks * TILE
+    locals_count = weights_ref.shape[0]
+    step = blocks // PROJECT_PARTS
+    slots = step * TILE
     upper = lax.broadcasted_iota(jnp.int32, (slots, 1), 0) % TILE < TILE // 2
 
-    def tile_rows(tile):
-        return jnp.concatenate(
-            [rows_ref[m, :, tile].reshape(slots, -1) for m in range(parts)], axis=1
+    def load_rows(part):
+        here = pl.ds(part * step, step)
+        return pltpu.make_async_copy(
+            rows_hbm.at[:, here], rows_ref.at[:, here], row_sems.at[part]
         )
 
-    ends = tile_rows(2)
-    none = jnp.zeros_like(ends)
-    mixed = None
-    for local in range(2):
-        end = jnp.where(upper, ends, none) if local == 0 else jnp.where(upper, none, ends)
-        rows = jnp.concatenate([tile_rows(local), end], axis=0)
-        value = dot(rows, weights_ref[local])
-        out_ref[:, local] = value[:slots].astype(BF16).reshape(blocks, TILE, width)
-        mixed = value[slots:] if mixed is None else mixed + value[slots:]
-    out_ref[:, 2] = mixed.astype(BF16).reshape(blocks, TILE, width)
+    def load_weights(local):
+        return pltpu.make_async_copy(
+            weights_hbm.at[local], weights_ref.at[local], weight_sems.at[local]
+        )
+
+    loads = [load_rows(0), load_weights(0)]
+    loads += [load_rows(part) for part in range(1, PROJECT_PARTS)]
+    loads += [load_weights(local) for local in range(1, locals_count)]
+    for load in loads:
+        load.start()
+    stores = []
+
+    def store(part, tile):
+        here = pl.ds(part * step, step)
+        copy = pltpu.make_async_copy(
+            out_ref.at[here, tile], out_hbm.at[here, tile], out_sems.at[part, tile]
+        )
+        copy.start()
+        stores.append(copy)
+
+    for local in range(locals_count):
+        for part in range(PROJECT_PARTS):
+            here = slice(part * step, (part + 1) * step)
+            if local == 0:
+                load_rows(part).wait()
+            if part == 0:
+                load_weights(local).wait()
+
+            def tile_rows(tile, here=here):
+                return jnp.concatenate(
+                    [rows_ref[m, here, tile].reshape(slots, -1) for m in range(parts)], axis=1
+                )
+
+            ends = tile_rows(2)
+            none = jnp.zeros_like(ends)
+            end = jnp.where(upper, ends, none) if local == 0 else jnp.where(upper, none, ends)
+            rows = jnp.concatenate([tile_rows(local), end], axis=0)
+            value = dot(rows, weights_ref[local])
+            out_ref[here, local] = value[:slots].astype(BF16).reshape(step, TILE, width)
+            store(part, local)
+            if local == 0:
+                mixed_ref[part] = value[slots:]
+            else:
+                mixed = mixed_ref[part] + value[slots:]
+                out_ref[here, 2] = mixed.astype(BF16).reshape(step, TILE, width)
+                store(part, 2)
+    for copy in stores:
+        copy.wait()
 
 
 def project_rows(rows, weights):
     parts, blocks, _, _, hidden_part = rows.shape
     width = weights.shape[2]
-    step = PROJECT_STEP
+    shape = (blocks, HELD, TILE, width)
     return pl.pallas_call(
         project_kernel,
-        out_shape=jax.ShapeDtypeStruct((blocks, HELD, TILE, width), BF16),
-        grid=(blocks // step,),
-        in_specs=[
-            pl.BlockSpec((parts, step, HELD, TILE, hidden_part), lambda i: (0, i, 0, 0, 0)),
-            pl.BlockSpec(weights.shape, lambda i: (0, 0, 0)),
+        out_shape=pltpu.HBM(shape, BF16),
+        in_specs=[pl.BlockSpec(memory_space=pl.ANY)] * 2,
+        out_specs=pl.BlockSpec(memory_space=pltpu.HBM),
+        scratch_shapes=[
+            pltpu.VMEM(rows.shape, BF16),
+            pltpu.VMEM(weights.shape, BF16),
+            pltpu.VMEM(shape, BF16),
+            pltpu.VMEM((PROJECT_PARTS, blocks // PROJECT_PARTS * TILE, width), F32),
+            pltpu.SemaphoreType.DMA((PROJECT_PARTS,)),
+            pltpu.SemaphoreType.DMA((weights.shape[0],)),
+            pltpu.SemaphoreType.DMA((PROJECT_PARTS, HELD)),
         ],
-        out_specs=pl.BlockSpec((step, HELD, TILE, width), lambda i: (i, 0, 0, 0)),
         compiler_params=pltpu.CompilerParams(vmem_limit_bytes=VMEM_GRANT),
         cost_estimate=pl.CostEstimate(
             flops=4_000_000_000, bytes_accessed=10_000_000, transcendentals=0
@@ -230,7 +286,7 @@
     tiles = KEPT * (width // LANES) + KEPT
     return pl.pallas_call(
         regroup_kernel,
-        out_shape=jax.ShapeDtypeStruct((group_count, tiles, TILE, LANES), BF16),
+        out_shape=pltpu.HBM((group_count, tiles, TILE, LANES), BF16),
         in_specs=[
             pl.BlockSpec(memory_space=pltpu.SMEM),
             pl.BlockSpec(memory_space=pltpu.VMEM),
@@ -344,7 +400,9 @@
     )(rows, after)
 
 
-def merge_kernel(packed_hbm, maps_hbm, out_ref, packed_ref, maps_ref, rows_ref, sems):
+def merge_kernel(
+    packed_hbm, maps_hbm, out_hbm, packed_ref, maps_ref, rows_ref, out_ref, sems, out_sems
+):
     groups = packed_ref.shape[0]
     size, width = out_ref.shape
     blocks = width // LANES
@@ -368,11 +426,18 @@
         if block >= KEPT:
             last = pltpu.roll(last.astype(F32), ends - TILE // 2, 0).astype(BF16)
         rows_ref[kept:, lanes] = last
+    stores = []
     for index, copy in enumerate(copies):
         copy.wait()
         value = dot(maps_ref[2 * index * BLK : 2 * (index + 1) * BLK], rows_ref[...])
         here = slice(index * BLK, (index + 1) * BLK)
         out_ref[here] = (value[:BLK] + value[BLK:]).astype(BF16)
+        stores.append(
+            pltpu.make_async_copy(out_ref.at[here], out_hbm.at[here], out_sems.at[index])
+        )
+        stores[-1].start()
+    for store in stores:
+        store.wait()
 
 
 def merge_rows(packed, maps):
@@ -380,14 +445,16 @@
     width = (packed.shape[1] // KEPT - 1) * LANES
     return pl.pallas_call(
         merge_kernel,
-        out_shape=jax.ShapeDtypeStruct((size // 2, width), BF16),
+        out_shape=pltpu.HBM((size // 2, width), BF16),
         in_specs=[pl.BlockSpec(memory_space=pl.ANY)] * 2,
-        out_specs=pl.BlockSpec(memory_space=pltpu.VMEM),
+        out_specs=pl.BlockSpec(memory_space=pltpu.HBM),
         scratch_shapes=[
             pltpu.VMEM(packed.shape, BF16),
             pltpu.VMEM(maps.shape, BF16),
             pltpu.VMEM((slots, width), BF16),
+            pltpu.VMEM((size // 2, width), BF16),
             pltpu.SemaphoreType.DMA((1 + size // (2 * BLK),)),
+            pltpu.SemaphoreType.DMA((size // (2 * BLK),)),
         ],
         compiler_params=pltpu.CompilerParams(vmem_limit_bytes=VMEM_GRANT),
         cost_estimate=pl.CostEstimate(
@@ -447,7 +514,6 @@
     projected = project_rows(
         held.reshape(parts, group_count, HELD, TILE, hidden_part), down_proj
     )
-    at_owner, projected = lax.optimization_barrier((at_owner, projected))
     home = exchange(projected.reshape(group_count, HELD * TILE, out_part))
     owned = lax.all_gather(at_owner, "mp", axis=0)
     regrouped = regroup_rows(home.reshape(group_count, HELD, TILE, out_part), members)

time: 302 us -> 302 us (level)
    unnamed x13 -> x7, local copies, waits for them, and re-layouts: 5.78 us -> 2.75 us
  transfers between devices with their start and end apart: 6 -> 6, of which waited for: 4 -> 4; matrix products, arithmetic and copies ran while one was open for 0% -> 0% of each run, Pallas kernels for 29% -> 30%
where the time goes in v5:
time: 302 us; the launch traced here: 301 us
  waiting for transfers between devices  137 us (45%)
  Pallas kernels  109 us (36%)
  starting transfers between devices  35.9 us (12%)
  between operations  13.5 us (4%)
  local copies, waits for them, and re-layouts  4.9 us (2%)
    all_to_all x4, waiting for transfers between devices, exchange(): lax.all_to_all(rows, 'expert', split_axis=0, concat_axis=0, tiled=True)  103 us
    pallas_call x1, Pallas kernels, invert_gram(): pl.pallas_call(invert_kernel, out_shape=jax.ShapeDtypeStruct((2 * width,...  72.9 us
    all_to_all x4, starting transfers between devices, exchange(): lax.all_to_all(rows, 'expert', split_axis=0, concat_axis=0, tiled=True)  35.8 us
    all_gather x1, waiting for transfers between devices, on_device(): held = lax.all_gather(at_holder, 'mp', axis=0)  33.1 us
    pallas_call x1, Pallas kernels, merge_rows(): pl.pallas_call(merge_kernel, out_shape=pltpu.HBM((size // 2, width), BF16...  15.3 us
    pallas_call x2, Pallas kernels, pack_rows(): pl.pallas_call(slot_kernel, out_shape=jax.ShapeDtypeStruct((slots, width)...  10.6 us
    pallas_call x1, Pallas kernels, project_rows(): pl.pallas_call(project_kernel, out_shape=pltpu.HBM(shape, BF16), in_specs...  7.73 us
  transfers between devices with their start and end apart: 6, of which 4 were waited for; matrix products, arithmetic and copies ran while one was open for 0% of the time, Pallas kernels for 30%

profile of v5, /device:TPU:1, one launch (start us, length us, event | category | flops | bytes accessed | tf_op | source)
XLA Modules:
  0.0 301.1 jit_solution(10370202091200852561)
XLA Ops:
  6.5 0.8 copy.14
  7.3 0.7 reshape.101.routes_ref
  8.0 0.7 copy.15.bases_ref
  8.8 0.0 copy-start.2
  8.8 4.6 %pack_held.1 = bf16[1536,256]{1,0:T(8,128)(2,1)} custom-call(s32[1,1024]{1,0:T(1,128)} %reshape.101.routes_ref, s32[128,2]{1,0:T(8,128)} %copy.15.bases_ref, bf16[1024,256]{1,0:T(8,128)(2,1)} %bitcast.18), custom_call_target="tpu_custom_call" | custom-call | flops 3000000000 | bytes 2000000 | tf_op jit(solution)/shard_map/pack_held/pallas_call | solution.py:123
  13.4 13.0 %all-to-all-start = ((bf16[64,24,256]{2,1,0:T(8,128)(2,1)}), bf16[64,24,256]{2,1,0:T(8,128)(2,1)S(1)}, u32[]{:S(2)}, u32[]{:S(2)}) async-start(bf16[64,24,256]{2,1,0:T(8,128)(2,1)} %bitcast.15), calls=%async_computation | async-start | bytes 1572864 | tf_op jit(solution)/shard_map/all_to_all | solution.py:483
  26.4 0.0 all-gather.5.cloned.1.call-start
  26.5 0.0 copy-done.2
  26.5 0.2 convert_reduce_fusion
  26.7 0.7 copy.16.bases_ref
  27.4 6.0 %pack_owned.1 = bf16[2560,256]{1,0:T(8,128)(2,1)} custom-call(s32[1,1024]{1,0:T(1,128)} %reshape.101.routes_ref, s32[128,2]{1,0:T(8,128)} %copy.16.bases_ref, bf16[1024,256]{1,0:T(8,128)(2,1)} %bitcast.19), custom_call_target="tpu_custom_call" | custom-call | flops 3000000000 | bytes 2000000 | tf_op jit(solution)/shard_map/pack_owned/pallas_call | solution.py:123
  33.4 16.0 %all-to-all-done = bf16[64,24,256]{2,1,0:T(8,128)(2,1)S(1)} async-done(((bf16[64,24,256]{2,1,0:T(8,128)(2,1)}), bf16[64,24,256]{2,1,0:T(8,128)(2,1)S(1)}, u32[]{:S(2)}, u32[]{:S(2)}) %all-to-all-start) | async-done | bytes 786464 | tf_op jit(solution)/shard_map/all_to_all | solution.py:483
  49.4 0.0 copy-start.1
  49.4 0.9 copy-done.1
  50.3 0.0 all-gather.5.cloned.1.call-update
  50.3 6.2 %all-to-all-start.3 = ((bf16[64,40,256]{2,1,0:T(8,128)(2,1)}), bf16[64,40,256]{2,1,0:T(8,128)(2,1)S(1)}, u32[]{:S(2)}, u32[]{:S(2)}) async-start(bf16[64,40,256]{2,1,0:T(8,128)(2,1)} %bitcast.14), calls=%async_computation.3 | async-start | bytes 2621440 | tf_op jit(solution)/shard_map/all_to_all | solution.py:483
  56.5 33.1 %all-gather.5.cloned.1.call-done = bf16[256,24,256]{2,1,0:T(8,128)(2,1)} async-done(((bf16[64,24,256]{2,1,0:T(8,128)(2,1)}), bf16[256,24,256]{2,1,0:T(8,128)(2,1)}) %all-gather.5.cloned.1.call-update) | async-done | bytes 3145744 | tf_op jit(solution)/shard_map/all_gather | solution.py:511
  89.6 7.7 %project_rows.1 = bf16[64,3,8,896]{3,2,1,0:T(8,128)(2,1)} custom-call(bf16[4,64,3,8,256]{4,3,2,1,0:T(8,128)(2,1)} %bitcast.17, bf16[2,1024,896]{2,1,0:T(8,128)(2,1)} %weights_hbm.1), custom_call_target="tpu_custom_call" | custom-call | flops 4000000000 | bytes 10000000 | tf_op jit(solution)/shard_map/project_rows/pallas_call | solution.py:212
  97.4 0.0 all-to-all-done.3
  97.4 0.0 copy-start
  97.4 1.0 copy-done
  98.4 10.7 %all-to-all-start.1 = ((bf16[64,24,896]{2,1,0:T(8,128)(2,1)}), bf16[64,24,896]{2,1,0:T(8,128)(2,1)S(1)}, u32[]{:S(2)}, u32[]{:S(2)}) async-start(bf16[64,24,896]{2,1,0:T(8,128)(2,1)} %bitcast.13), calls=%async_computation.1 | async-start | bytes 5505024 | tf_op jit(solution)/shard_map/all_to_all | solution.py:483
  109.1 0.0 all-gather.7.cloned.1.call-start
  109.1 0.7 all-gather.7.cloned.1.call-update
  109.9 0.1 select_reduce_fusion.members_ref
  110.0 64.2 %all-to-all-done.1 = bf16[64,24,896]{2,1,0:T(8,128)(2,1)S(1)} async-done(((bf16[64,24,896]{2,1,0:T(8,128)(2,1)}), bf16[64,24,896]{2,1,0:T(8,128)(2,1)S(1)}, u32[]{:S(2)}, u32[]{:S(2)}) %all-to-all-start.1) | async-done | bytes 2752544 | tf_op jit(solution)/shard_map/all_to_all | solution.py:483
  174.2 2.9 regroup_rows.1.after_ref
  177.0 5.9 %all-to-all-start.2 = ((bf16[64,32,8,128]{3,2,1,0:T(8,128)(2,1)}), bf16[64,32,8,128]{3,2,1,0:T(8,128)(2,1)}, u32[]{:S(2)}, u32[]{:S(2)}) async-start(bf16[64,32,8,128]{3,2,1,0:T(8,128)(2,1)} %regroup_rows.1.after_ref), calls=%async_computation.2 | async-start | bytes 8388608 | tf_op jit(solution)/shard_map/all_to_all | solution.py:483
  183.0 0.0 all-gather.7.cloned.1.call-done
  183.0 72.9 %invert_gram.1.maps_hbm = bf16[2048,2560]{1,0:T(8,128)(2,1)} custom-call(bf16[4,64,5,8,256]{4,3,2,1,0:T(8,128)(2,1)} %bitcast.16, bf16[64,32,8,128]{3,2,1,0:T(8,128)(2,1)} %regroup_rows.1.after_ref), custom_call_target="tpu_custom_call" | custom-call | flops 60000002048 | bytes 16000000 | tf_op jit(solution)/shard_map/invert_gram/pallas_call | solution.py:386
  255.9 23.0 %all-to-all-done.2.packed_hbm = bf16[64,32,8,128]{3,2,1,0:T(8,128)(2,1)} async-done(((bf16[64,32,8,128]{3,2,1,0:T(8,128)(2,1)}), bf16[64,32,8,128]{3,2,1,0:T(8,128)(2,1)}, u32[]{:S(2)}, u32[]{:S(2)}) %all-to-all-start.2) | async-done | bytes 4194336 | tf_op jit(solution)/shard_map/all_to_all | solution.py:483
  278.9 15.3 %merge_rows.1 = bf16[1024,896]{1,0:T(8,128)(2,1)} custom-call(bf16[64,32,8,128]{3,2,1,0:T(8,128)(2,1)} %all-to-all-done.2.packed_hbm, bf16[2048,2560]{1,0:T(8,128)(2,1)} %invert_gram.1.maps_hbm), custom_call_target="tpu_custom_call" | custom-call | flops 9400000512 | bytes 16000000 | tf_op jit(solution)/shard_map/merge_rows/pallas_call | solution.py:446
  (4 shorter events, 0.0 us)
Async XLA Ops:
  8.8 17.7 %copy-start.2 = (s32[128]{0:T(128)S(1)}, s32[128]{0:T(128)}, u32[]{:S(2)}) copy-start(s32[128]{0:T(128)} %param.7) | copy-start | bytes 1540
  13.4 36.0 %all-to-all-start = ((bf16[64,24,256]{2,1,0:T(8,128)(2,1)}), bf16[64,24,256]{2,1,0:T(8,128)(2,1)S(1)}, u32[]{:S(2)}, u32[]{:S(2)}) async-start(bf16[64,24,256]{2,1,0:T(8,128)(2,1)} %bitcast.15), calls=%async_computation | async-start | bytes 1572864 | tf_op jit(solution)/shard_map/all_to_all | solution.py:483
  26.4 63.2 %all-gather.5.cloned.1.call-start = ((), (), s32[]{:S(2)}) async-start(), calls=%async_computation.4 | async-start | bytes 3932160 | tf_op jit(solution)/shard_map/all_gather | solution.py:511
  49.4 0.9 copy-start.1
  50.3 47.0 %all-to-all-start.3 = ((bf16[64,40,256]{2,1,0:T(8,128)(2,1)}), bf16[64,40,256]{2,1,0:T(8,128)(2,1)S(1)}, u32[]{:S(2)}, u32[]{:S(2)}) async-start(bf16[64,40,256]{2,1,0:T(8,128)(2,1)} %bitcast.14), calls=%async_computation.3 | async-start | bytes 2621440 | tf_op jit(solution)/shard_map/all_to_all | solution.py:483
  97.4 1.1 copy-start
  98.4 75.7 %all-to-all-start.1 = ((bf16[64,24,896]{2,1,0:T(8,128)(2,1)}), bf16[64,24,896]{2,1,0:T(8,128)(2,1)S(1)}, u32[]{:S(2)}, u32[]{:S(2)}) async-start(bf16[64,24,896]{2,1,0:T(8,128)(2,1)} %bitcast.13), calls=%async_computation.1 | async-start | bytes 5505024 | tf_op jit(solution)/shard_map/all_to_all | solution.py:483
  109.1 73.9 %all-gather.7.cloned.1.call-start = ((), (), s32[]{:S(2)}) async-start(), calls=%async_computation.5 | async-start | bytes 6553600 | tf_op jit(solution)/shard_map/all_gather | solution.py:518
  177.0 101.8 %all-to-all-start.2 = ((bf16[64,32,8,128]{3,2,1,0:T(8,128)(2,1)}), bf16[64,32,8,128]{3,2,1,0:T(8,128)(2,1)}, u32[]{:S(2)}, u32[]{:S(2)}) async-start(bf16[64,32,8,128]{3,2,1,0:T(8,128)(2,1)} %regroup_rows.1.after_ref), calls=%async_computation.2 | async-start | bytes 8388608 | tf_op jit(solution)/shard_map/all_to_all | solution.py:483
Sparse Core Ops, SparseCore 0:
  50.5 39.1 all-gather.4
  111.8 59.3 all-gather.6

commit v6 on v5

--- a/solution.py
+++ b/solution.py
@@ -89,11 +89,11 @@
 UNROLL = 4
 PROJECT_PARTS = 2
 VMEM_GRANT = 58 * 1024 * 1024
-
-
-def slot_kernel(routes_ref, bases_ref, rows_hbm, out_ref, slot_ref, rows_ref, sem):
-    copy = pltpu.make_async_copy(rows_hbm, rows_ref, sem)
-    copy.start()
+WIDE_GRANT = 60 * 1024 * 1024
+SMALL_GRANT = 32 * 1024 * 1024
+
+
+def slot_kernel(routes_ref, bases_ref, rows_ref, out_ref, slot_ref):
     experts = bases_ref.shape[0]
     count = routes_ref.shape[1]
     hit = lax.broadcasted_iota(jnp.int32, (experts, count), 0) == routes_ref[...]
@@ -106,7 +106,6 @@
     place = before + jnp.where(before < TILE, bases[:, 0:1], bases[:, 1:2])
     slot = jnp.sum(jnp.where(hit, place, 0.0), axis=0, keepdims=True)
     slot_ref[...] = slot.astype(jnp.int32)
-    copy.wait()
 
     def fill(index, carry):
         here = pl.multiple_of(index * BLK, BLK)
@@ -118,20 +117,15 @@
     lax.fori_loop(0, out_ref.shape[0] // BLK, fill, 0)
 
 
-def pack_rows(routes, bases, rows, slots, name):
+def pack_rows(routes, bases, rows, slots, grant, name):
     count, width = rows.shape
     return pl.pallas_call(
         slot_kernel,
         out_shape=jax.ShapeDtypeStruct((slots, width), BF16),
-        in_specs=[pl.BlockSpec(memory_space=pltpu.VMEM)] * 2
-        + [pl.BlockSpec(memory_space=pl.ANY)],
+        in_specs=[pl.BlockSpec(memory_space=pltpu.VMEM)] * 3,
         out_specs=pl.BlockSpec(memory_space=pltpu.VMEM),
-        scratch_shapes=[
-            pltpu.VMEM((1, count), jnp.int32),
-            pltpu.VMEM(rows.shape, BF16),
-            pltpu.SemaphoreType.DMA,
-        ],
-        compiler_params=pltpu.CompilerParams(vmem_limit_bytes=VMEM_GRANT),
+        scratch_shapes=[pltpu.VMEM((1, count), jnp.int32)],
+        compiler_params=pltpu.CompilerParams(vmem_limit_bytes=grant),
         cost_estimate=pl.CostEstimate(
             flops=3_000_000_000, bytes_accessed=2_000_000, transcendentals=0
         ),
@@ -223,7 +217,7 @@
             pltpu.SemaphoreType.DMA((weights.shape[0],)),
             pltpu.SemaphoreType.DMA((PROJECT_PARTS, HELD)),
         ],
-        compiler_params=pltpu.CompilerParams(vmem_limit_bytes=VMEM_GRANT),
+        compiler_params=pltpu.CompilerParams(vmem_limit_bytes=WIDE_GRANT),
         cost_estimate=pl.CostEstimate(
             flops=4_000_000_000, bytes_accessed=10_000_000, transcendentals=0
         ),
@@ -304,12 +298,23 @@
     )(members, held)
 
 
+def pair_ends(first, second, lower):
+    shape = first.shape
+    first, second = (part.astype(F32).reshape(-1, shape[-1]) for part in (first, second))
+    upper = lax.broadcasted_iota(jnp.int32, first.shape, 0) % TILE < TILE // 2
+    if lower:
+        first = pltpu.roll(first, first.shape[0] - TILE // 2, 0)
+    else:
+        second = pltpu.roll(second, TILE // 2, 0)
+    return jnp.where(upper, first, second).astype(BF16)
+
+
 def invert_kernel(rows_ref, after_ref, maps_ref, turned_ref, sys_ref):
     del after_ref
     count, blocks = rows_ref.shape[:2]
     width = count * BLK
     kept = blocks * KEPT * TILE
-    ends = blocks * TILE
+    ends = blocks * TILE // 2
     diag = lax.broadcasted_iota(jnp.int32, (BLK, BLK), 0) == lax.broadcasted_iota(
         jnp.int32, (BLK, BLK), 1
     )
@@ -317,10 +322,13 @@
     def span(index):
         return pl.ds(pl.multiple_of(index * BLK, BLK), BLK)
 
+    def end_rows(i):
+        last = rows_ref[i, :, KEPT].reshape(blocks // 2, 2, TILE, BLK)
+        return pair_ends(last[:, 0], last[:, 1], False)
+
     def turn(i, carry):
         turned_ref[span(i), :kept] = rows_ref[i, :, :KEPT].reshape(kept, BLK).T
-        last = rows_ref[i, :, KEPT].reshape(ends, BLK)
-        turned_ref[span(i), kept:] = last.T
+        turned_ref[span(i), kept:] = end_rows(i).T
         return carry
 
     lax.fori_loop(0, count, turn, 0)
@@ -328,8 +336,7 @@
     def gram_block(index, carry):
         i, j = index // count, index % count
         value = dot(turned_ref[span(i), :kept], rows_ref[j, :, :KEPT].reshape(kept, BLK))
-        last = rows_ref[j, :, KEPT].reshape(ends, BLK)
-        sys_ref[span(i), span(j)] = value + dot(turned_ref[span(i), kept:], last)
+        sys_ref[span(i), span(j)] = value + dot(turned_ref[span(i), kept:], end_rows(j))
         return carry
 
     lax.fori_loop(0, count * count, gram_block, 0)
@@ -374,7 +381,7 @@
         maps_ref[span(2 * i + 1), here] = low
         return carry
 
-    strip = 2 * BLK
+    strip = 3 * BLK
     strips = (kept + ends) // strip
     lax.fori_loop(0, count * strips, map_block, 0)
 
@@ -382,7 +389,7 @@
 def invert_gram(rows, after):
     count, blocks, _, _, _ = rows.shape
     width = count * BLK
-    slots = blocks * TILE * OWNED
+    slots = blocks * TILE * KEPT + blocks * TILE // 2
     return pl.pallas_call(
         invert_kernel,
         out_shape=jax.ShapeDtypeStruct((2 * width, slots), BF16),
@@ -407,7 +414,6 @@
     size, width = out_ref.shape
     blocks = width // LANES
     kept = groups * KEPT * TILE
-    ends = groups * TILE
     first = pltpu.make_async_copy(packed_hbm, packed_ref, sems.at[0])
     first.start()
     copies = []
@@ -422,10 +428,9 @@
         lanes = slice(block * LANES, (block + 1) * LANES)
         rows = packed_ref[:, KEPT * block : KEPT * block + KEPT]
         rows_ref[:kept, lanes] = rows.reshape(kept, LANES)
-        last = packed_ref[:, KEPT * blocks + block % KEPT].reshape(ends, LANES)
-        if block >= KEPT:
-            last = pltpu.roll(last.astype(F32), ends - TILE // 2, 0).astype(BF16)
-        rows_ref[kept:, lanes] = last
+        last = packed_ref[:, KEPT * blocks + block % KEPT]
+        last = last.reshape(groups // 2, 2, TILE, LANES)
+        rows_ref[kept:, lanes] = pair_ends(last[:, 0], last[:, 1], block >= KEPT)
     stores = []
     for index, copy in enumerate(copies):
         copy.wait()
@@ -501,10 +506,10 @@
     members, owned_bases = member_places(merge_group, group_count)
 
     to_holder = pack_rows(
-        targets, held_bases, rows, group_count * HELD * TILE, "pack_held"
+        targets, held_bases, rows, group_count * HELD * TILE, SMALL_GRANT, "pack_held"
     ).reshape(group_count, HELD * TILE, hidden_part)
     to_owner = pack_rows(
-        targets, owned_bases, rows, group_count * OWNED * TILE, "pack_owned"
+        targets, owned_bases, rows, group_count * OWNED * TILE, WIDE_GRANT, "pack_owned"
     ).reshape(group_count, OWNED * TILE, hidden_part)
     at_holder = exchange(to_holder)
     at_holder, to_owner = lax.optimization_barrier((at_holder, to_owner))

time: 302 us -> 299 us (0.990)
  Pallas kernels: 109 us -> 103 us
  waiting for transfers between devices: 137 us -> 141 us
    all_to_all x4, waiting for transfers between devices: 103 us -> 107 us  [exchange(): lax.all_to_all(rows, 'expert', split_axis=0, concat_axis=0, tiled=True)]
    pallas_call x1, Pallas kernels: 72.9 us -> 68.9 us  [invert_gram(): pl.pallas_call(invert_kernel, out_shape=jax.ShapeDtypeStruct((2 * width,...]
  transfers between devices with their start and end apart: 6 -> 6, of which waited for: 4 -> 4; matrix products, arithmetic and copies ran while one was open for 0% -> 0% of each run, Pallas kernels for 30% -> 29%
where the time goes in v6:
time: 299 us; the launch traced here: 298 us
  waiting for transfers between devices  141 us (47%)
  Pallas kernels  103 us (34%)
  starting transfers between devices  35.9 us (12%)
  between operations  13.5 us (5%)
  local copies, waits for them, and re-layouts  4.73 us (2%)
    all_to_all x4, waiting for transfers between devices, exchange(): lax.all_to_all(rows, 'expert', split_axis=0, concat_axis=0, tiled=True)  107 us
    pallas_call x1, Pallas kernels, invert_gram(): pl.pallas_call(invert_kernel, out_shape=jax.ShapeDtypeStruct((2 * width,...  68.9 us
    all_to_all x4, starting transfers between devices, exchange(): lax.all_to_all(rows, 'expert', split_axis=0, concat_axis=0, tiled=True)  35.8 us
    all_gather x1, waiting for transfers between devices, on_device(): held = lax.all_gather(at_holder, 'mp', axis=0)  33.1 us
    pallas_call x1, Pallas kernels, merge_rows(): pl.pallas_call(merge_kernel, out_shape=pltpu.HBM((size // 2, width), BF16...  14.3 us
    pallas_call x2, Pallas kernels, pack_rows(): pl.pallas_call(slot_kernel, out_shape=jax.ShapeDtypeStruct((slots, width)...  8.9 us
    pallas_call x1, Pallas kernels, project_rows(): pl.pallas_call(project_kernel, out_shape=pltpu.HBM(shape, BF16), in_specs...  7.7 us
  transfers between devices with their start and end apart: 6, of which 4 were waited for; matrix products, arithmetic and copies ran while one was open for 0% of the time, Pallas kernels for 29%

profile of v6, /device:TPU:1, one launch (start us, length us, event | category | flops | bytes accessed | tf_op | source)
XLA Modules:
  0.0 298.4 jit_solution(2261920022828034817)
XLA Ops:
  6.5 0.8 copy.14
  7.3 0.1 reshape.101.routes_ref
  7.5 0.1 copy.15.bases_ref
  7.6 1.0 copy-done.1
  8.6 3.2 %pack_held.1 = bf16[1536,256]{1,0:T(8,128)(2,1)} custom-call(s32[1,1024]{1,0:T(1,128)S(1)} %reshape.101.routes_ref, s32[128,2]{1,0:T(8,128)S(1)} %copy.15.bases_ref, bf16[1024,256]{1,0:T(8,128)(2,1)S(1)} %bitcast.14), custom_call_target="tpu_custom_call" | custom-call | flops 3000000000 | bytes 2000000 | tf_op jit(solution)/shard_map/pack_held/pallas_call | solution.py:122
  11.8 0.0 copy-done
  11.8 13.0 %all-to-all-start = ((bf16[64,24,256]{2,1,0:T(8,128)(2,1)}), bf16[64,24,256]{2,1,0:T(8,128)(2,1)S(1)}, u32[]{:S(2)}, u32[]{:S(2)}) async-start(bf16[64,24,256]{2,1,0:T(8,128)(2,1)} %bitcast.1), calls=%async_computation | async-start | bytes 1572864 | tf_op jit(solution)/shard_map/all_to_all | solution.py:488
  24.8 0.0 all-gather.5.cloned.1.call-start
  24.9 0.0 copy-done.4
  24.9 0.2 convert_reduce_fusion
  25.1 0.7 copy.16.bases_ref
  25.8 5.7 %pack_owned.1 = bf16[2560,256]{1,0:T(8,128)(2,1)} custom-call(s32[1,1024]{1,0:T(1,128)} %copy-done, s32[128,2]{1,0:T(8,128)} %copy.16.bases_ref, bf16[1024,256]{1,0:T(8,128)(2,1)} %bitcast.13), custom_call_target="tpu_custom_call" | custom-call | flops 3000000000 | bytes 2000000 | tf_op jit(solution)/shard_map/pack_owned/pallas_call | solution.py:122
  31.5 16.3 %all-to-all-done = bf16[64,24,256]{2,1,0:T(8,128)(2,1)S(1)} async-done(((bf16[64,24,256]{2,1,0:T(8,128)(2,1)}), bf16[64,24,256]{2,1,0:T(8,128)(2,1)S(1)}, u32[]{:S(2)}, u32[]{:S(2)}) %all-to-all-start) | async-done | bytes 786464 | tf_op jit(solution)/shard_map/all_to_all | solution.py:488
  47.8 0.9 copy-done.3
  48.7 0.0 all-gather.5.cloned.1.call-update
  48.7 6.2 %all-to-all-start.3 = ((bf16[64,40,256]{2,1,0:T(8,128)(2,1)}), bf16[64,40,256]{2,1,0:T(8,128)(2,1)S(1)}, u32[]{:S(2)}, u32[]{:S(2)}) async-start(bf16[64,40,256]{2,1,0:T(8,128)(2,1)} %bitcast.16), calls=%async_computation.3 | async-start | bytes 2621440 | tf_op jit(solution)/shard_map/all_to_all | solution.py:488
  55.0 33.1 %all-gather.5.cloned.1.call-done = bf16[256,24,256]{2,1,0:T(8,128)(2,1)} async-done(((bf16[64,24,256]{2,1,0:T(8,128)(2,1)}), bf16[256,24,256]{2,1,0:T(8,128)(2,1)}) %all-gather.5.cloned.1.call-update) | async-done | bytes 3145744 | tf_op jit(solution)/shard_map/all_gather | solution.py:516
  88.0 7.7 %project_rows.1 = bf16[64,3,8,896]{3,2,1,0:T(8,128)(2,1)} custom-call(bf16[4,64,3,8,256]{4,3,2,1,0:T(8,128)(2,1)} %bitcast.18, bf16[2,1024,896]{2,1,0:T(8,128)(2,1)} %weights_hbm.1), custom_call_target="tpu_custom_call" | custom-call | flops 4000000000 | bytes 10000000 | tf_op jit(solution)/shard_map/project_rows/pallas_call | solution.py:206
  95.7 0.0 all-to-all-done.3
  95.8 0.0 copy-start.2
  95.8 1.0 copy-done.2
  96.8 10.7 %all-to-all-start.1 = ((bf16[64,24,896]{2,1,0:T(8,128)(2,1)}), bf16[64,24,896]{2,1,0:T(8,128)(2,1)S(1)}, u32[]{:S(2)}, u32[]{:S(2)}) async-start(bf16[64,24,896]{2,1,0:T(8,128)(2,1)} %bitcast.15), calls=%async_computation.1 | async-start | bytes 5505024 | tf_op jit(solution)/shard_map/all_to_all | solution.py:488
  107.5 0.0 all-gather.7.cloned.1.call-start
  107.5 0.7 all-gather.7.cloned.1.call-update
  108.2 0.1 select_reduce_fusion.members_ref
  108.3 64.2 %all-to-all-done.1 = bf16[64,24,896]{2,1,0:T(8,128)(2,1)S(1)} async-done(((bf16[64,24,896]{2,1,0:T(8,128)(2,1)}), bf16[64,24,896]{2,1,0:T(8,128)(2,1)S(1)}, u32[]{:S(2)}, u32[]{:S(2)}) %all-to-all-start.1) | async-done | bytes 2752544 | tf_op jit(solution)/shard_map/all_to_all | solution.py:488
  172.6 2.9 regroup_rows.1.after_ref
  175.5 5.9 %all-to-all-start.2 = ((bf16[64,32,8,128]{3,2,1,0:T(8,128)(2,1)}), bf16[64,32,8,128]{3,2,1,0:T(8,128)(2,1)}, u32[]{:S(2)}, u32[]{:S(2)}) async-start(bf16[64,32,8,128]{3,2,1,0:T(8,128)(2,1)} %regroup_rows.1.after_ref), calls=%async_computation.2 | async-start | bytes 8388608 | tf_op jit(solution)/shard_map/all_to_all | solution.py:488
  181.4 0.0 all-gather.7.cloned.1.call-done
  181.4 68.9 %invert_gram.1.maps_hbm = bf16[2048,2304]{1,0:T(8,128)(2,1)} custom-call(bf16[4,64,5,8,256]{4,3,2,1,0:T(8,128)(2,1)} %bitcast.17, bf16[64,32,8,128]{3,2,1,0:T(8,128)(2,1)} %regroup_rows.1.after_ref), custom_call_target="tpu_custom_call" | custom-call | flops 60000002048 | bytes 16000000 | tf_op jit(solution)/shard_map/invert_gram/pallas_call | solution.py:393
  250.4 26.9 %all-to-all-done.2.packed_hbm = bf16[64,32,8,128]{3,2,1,0:T(8,128)(2,1)} async-done(((bf16[64,32,8,128]{3,2,1,0:T(8,128)(2,1)}), bf16[64,32,8,128]{3,2,1,0:T(8,128)(2,1)}, u32[]{:S(2)}, u32[]{:S(2)}) %all-to-all-start.2) | async-done | bytes 4194336 | tf_op jit(solution)/shard_map/all_to_all | solution.py:488
  277.3 14.3 %merge_rows.1 = bf16[1024,896]{1,0:T(8,128)(2,1)} custom-call(bf16[64,32,8,128]{3,2,1,0:T(8,128)(2,1)} %all-to-all-done.2.packed_hbm, bf16[2048,2304]{1,0:T(8,128)(2,1)} %invert_gram.1.maps_hbm), custom_call_target="tpu_custom_call" | custom-call | flops 9400000512 | bytes 16000000 | tf_op jit(solution)/shard_map/merge_rows/pallas_call | solution.py:451
  (8 shorter events, 0.0 us)
Async XLA Ops:
  7.4 4.4 %copy-start = (s32[1,1024]{1,0:T(1,128)}, s32[1,1024]{1,0:T(1,128)S(1)}, u32[]{:S(2)}) copy-start(s32[1,1024]{1,0:T(1,128)S(1)} %reshape.101.routes_ref) | copy-start | bytes 12292
  7.6 1.0 copy-start.1
  8.6 16.3 %copy-start.4 = (s32[128]{0:T(128)S(1)}, s32[128]{0:T(128)}, u32[]{:S(2)}) copy-start(s32[128]{0:T(128)} %param.7) | copy-start | bytes 1540
  11.8 36.0 %all-to-all-start = ((bf16[64,24,256]{2,1,0:T(8,128)(2,1)}), bf16[64,24,256]{2,1,0:T(8,128)(2,1)S(1)}, u32[]{:S(2)}, u32[]{:S(2)}) async-start(bf16[64,24,256]{2,1,0:T(8,128)(2,1)} %bitcast.1), calls=%async_computation | async-start | bytes 1572864 | tf_op jit(solution)/shard_map/all_to_all | solution.py:488
  24.8 63.2 %all-gather.5.cloned.1.call-start = ((), (), s32[]{:S(2)}) async-start(), calls=%async_computation.4 | async-start | bytes 3932160 | tf_op jit(solution)/shard_map/all_gather | solution.py:516
  47.8 0.9 copy-start.3
  48.7 47.0 %all-to-all-start.3 = ((bf16[64,40,256]{2,1,0:T(8,128)(2,1)}), bf16[64,40,256]{2,1,0:T(8,128)(2,1)S(1)}, u32[]{:S(2)}, u32[]{:S(2)}) async-start(bf16[64,40,256]{2,1,0:T(8,128)(2,1)} %bitcast.16), calls=%async_computation.3 | async-start | bytes 2621440 | tf_op jit(solution)/shard_map/all_to_all | solution.py:488
  95.8 1.1 copy-start.2
  96.8 75.7 %all-to-all-start.1 = ((bf16[64,24,896]{2,1,0:T(8,128)(2,1)}), bf16[64,24,896]{2,1,0:T(8,128)(2,1)S(1)}, u32[]{:S(2)}, u32[]{:S(2)}) async-start(bf16[64,24,896]{2,1,0:T(8,128)(2,1)} %bitcast.15), calls=%async_computation.1 | async-start | bytes 5505024 | tf_op jit(solution)/shard_map/all_to_all | solution.py:488
  107.5 74.0 %all-gather.7.cloned.1.call-start = ((), (), s32[]{:S(2)}) async-start(), calls=%async_computation.5 | async-start | bytes 6553600 | tf_op jit(solution)/shard_map/all_gather | solution.py:523
  175.5 101.8 %all-to-all-start.2 = ((bf16[64,32,8,128]{3,2,1,0:T(8,128)(2,1)}), bf16[64,32,8,128]{3,2,1,0:T(8,128)(2,1)}, u32[]{:S(2)}, u32[]{:S(2)}) async-start(bf16[64,32,8,128]{3,2,1,0:T(8,128)(2,1)} %regroup_rows.1.after_ref), calls=%async_computation.2 | async-start | bytes 8388608 | tf_op jit(solution)/shard_map/all_to_all | solution.py:488
Sparse Core Ops, SparseCore 0:
  48.9 39.1 all-gather.4
  110.1 59.3 all-gather.6

commit v7 on v6

--- a/solution.py
+++ b/solution.py
@@ -408,29 +408,40 @@
 
 
 def merge_kernel(
-    packed_hbm, maps_hbm, out_hbm, packed_ref, maps_ref, rows_ref, out_ref, sems, out_sems
+    packed_hbm, maps_hbm, out_hbm, packed_ref, maps_ref, rows_ref, out_ref, sems, half_sems, out_sems
 ):
     groups = packed_ref.shape[0]
     size, width = out_ref.shape
     blocks = width // LANES
     kept = groups * KEPT * TILE
-    first = pltpu.make_async_copy(packed_hbm, packed_ref, sems.at[0])
-    first.start()
+    arrivals = []
+    for half in range(2):
+        here = pl.ds(half * (groups // 2), groups // 2)
+        arrivals.append(
+            pltpu.make_async_copy(packed_hbm.at[here], packed_ref.at[here], half_sems.at[half])
+        )
+        arrivals[-1].start()
     copies = []
     for index in range(size // BLK):
         here = slice(2 * index * BLK, 2 * (index + 1) * BLK)
         copies.append(
-            pltpu.make_async_copy(maps_hbm.at[here], maps_ref.at[here], sems.at[index + 1])
+            pltpu.make_async_copy(maps_hbm.at[here], maps_ref.at[here], sems.at[index])
         )
         copies[-1].start()
-    first.wait()
-    for block in range(blocks):
-        lanes = slice(block * LANES, (block + 1) * LANES)
-        rows = packed_ref[:, KEPT * block : KEPT * block + KEPT]
-        rows_ref[:kept, lanes] = rows.reshape(kept, LANES)
-        last = packed_ref[:, KEPT * blocks + block % KEPT]
-        last = last.reshape(groups // 2, 2, TILE, LANES)
-        rows_ref[kept:, lanes] = pair_ends(last[:, 0], last[:, 1], block >= KEPT)
+    count = groups // 2
+    tall = kept // 2
+    short = count * TILE // 2
+    for half, arrival in enumerate(arrivals):
+        arrival.wait()
+        here = slice(half * count, (half + 1) * count)
+        for block in range(blocks):
+            lanes = slice(block * LANES, (block + 1) * LANES)
+            rows = packed_ref[here, KEPT * block : KEPT * block + KEPT]
+            rows_ref[half * tall : (half + 1) * tall, lanes] = rows.reshape(tall, LANES)
+            last = packed_ref[here, KEPT * blocks + block % KEPT]
+            last = last.reshape(count // 2, 2, TILE, LANES)
+            at = kept + half * short
+            rows_ref[at : at + short, lanes] = pair_ends(last[:, 0], last[:, 1], block >= KEPT)
     stores = []
     for index, copy in enumerate(copies):
         copy.wait()
@@ -458,7 +469,8 @@
             pltpu.VMEM(maps.shape, BF16),
             pltpu.VMEM((slots, width), BF16),
             pltpu.VMEM((size // 2, width), BF16),
-            pltpu.SemaphoreType.DMA((1 + size // (2 * BLK),)),
+            pltpu.SemaphoreType.DMA((size // (2 * BLK),)),
+            pltpu.SemaphoreType.DMA((2,)),
             pltpu.SemaphoreType.DMA((size // (2 * BLK),)),
         ],
         compiler_params=pltpu.CompilerParams(vmem_limit_bytes=VMEM_GRANT),

time: 299 us -> 301 us (level)
  no operation moved by 1% of the time
where the time goes in v7:
time: 301 us; the launch traced here: 300 us
  waiting for transfers between devices  141 us (47%)
  Pallas kernels  105 us (35%)
  starting transfers between devices  35.9 us (12%)
  between operations  13.5 us (4%)
  local copies, waits for them, and re-layouts  4.73 us (2%)
    all_to_all x4, waiting for transfers between devices, exchange(): lax.all_to_all(rows, 'expert', split_axis=0, concat_axis=0, tiled=True)  107 us
    pallas_call x1, Pallas kernels, invert_gram(): pl.pallas_call(invert_kernel, out_shape=jax.ShapeDtypeStruct((2 * width,...  69.7 us
    all_to_all x4, starting transfers between devices, exchange(): lax.all_to_all(rows, 'expert', split_axis=0, concat_axis=0, tiled=True)  35.8 us
    all_gather x1, waiting for transfers between devices, on_device(): held = lax.all_gather(at_holder, 'mp', axis=0)  33.1 us
    pallas_call x1, Pallas kernels, merge_rows(): pl.pallas_call(merge_kernel, out_shape=pltpu.HBM((size // 2, width), BF16...  15.9 us
    pallas_call x2, Pallas kernels, pack_rows(): pl.pallas_call(slot_kernel, out_shape=jax.ShapeDtypeStruct((slots, width)...  8.9 us
    pallas_call x1, Pallas kernels, project_rows(): pl.pallas_call(project_kernel, out_shape=pltpu.HBM(shape, BF16), in_specs...  7.7 us
  transfers between devices with their start and end apart: 6, of which 4 were waited for; matrix products, arithmetic and copies ran while one was open for 0% of the time, Pallas kernels for 29%

profile of v7, /device:TPU:1, one launch (start us, length us, event | category | flops | bytes accessed | tf_op | source)
XLA Modules:
  0.0 300.1 jit_solution(47903216122322258)
XLA Ops:
  6.5 0.8 copy.14
  7.3 0.1 reshape.101.routes_ref
  7.5 0.1 copy.15.bases_ref
  7.6 1.0 copy-done.1
  8.6 3.2 %pack_held.1 = bf16[1536,256]{1,0:T(8,128)(2,1)} custom-call(s32[1,1024]{1,0:T(1,128)S(1)} %reshape.101.routes_ref, s32[128,2]{1,0:T(8,128)S(1)} %copy.15.bases_ref, bf16[1024,256]{1,0:T(8,128)(2,1)S(1)} %bitcast.14), custom_call_target="tpu_custom_call" | custom-call | flops 3000000000 | bytes 2000000 | tf_op jit(solution)/shard_map/pack_held/pallas_call | solution.py:122
  11.8 0.0 copy-done
  11.8 13.0 %all-to-all-start = ((bf16[64,24,256]{2,1,0:T(8,128)(2,1)}), bf16[64,24,256]{2,1,0:T(8,128)(2,1)S(1)}, u32[]{:S(2)}, u32[]{:S(2)}) async-start(bf16[64,24,256]{2,1,0:T(8,128)(2,1)} %bitcast.1), calls=%async_computation | async-start | bytes 1572864 | tf_op jit(solution)/shard_map/all_to_all | solution.py:500
  24.8 0.0 all-gather.5.cloned.1.call-start
  24.9 0.0 copy-done.4
  24.9 0.2 convert_reduce_fusion
  25.1 0.7 copy.16.bases_ref
  25.8 5.7 %pack_owned.1 = bf16[2560,256]{1,0:T(8,128)(2,1)} custom-call(s32[1,1024]{1,0:T(1,128)} %copy-done, s32[128,2]{1,0:T(8,128)} %copy.16.bases_ref, bf16[1024,256]{1,0:T(8,128)(2,1)} %bitcast.13), custom_call_target="tpu_custom_call" | custom-call | flops 3000000000 | bytes 2000000 | tf_op jit(solution)/shard_map/pack_owned/pallas_call | solution.py:122
  31.5 16.3 %all-to-all-done = bf16[64,24,256]{2,1,0:T(8,128)(2,1)S(1)} async-done(((bf16[64,24,256]{2,1,0:T(8,128)(2,1)}), bf16[64,24,256]{2,1,0:T(8,128)(2,1)S(1)}, u32[]{:S(2)}, u32[]{:S(2)}) %all-to-all-start) | async-done | bytes 786464 | tf_op jit(solution)/shard_map/all_to_all | solution.py:500
  47.8 0.9 copy-done.3
  48.7 0.0 all-gather.5.cloned.1.call-update
  48.7 6.2 %all-to-all-start.3 = ((bf16[64,40,256]{2,1,0:T(8,128)(2,1)}), bf16[64,40,256]{2,1,0:T(8,128)(2,1)S(1)}, u32[]{:S(2)}, u32[]{:S(2)}) async-start(bf16[64,40,256]{2,1,0:T(8,128)(2,1)} %bitcast.16), calls=%async_computation.3 | async-start | bytes 2621440 | tf_op jit(solution)/shard_map/all_to_all | solution.py:500
  55.0 33.1 %all-gather.5.cloned.1.call-done = bf16[256,24,256]{2,1,0:T(8,128)(2,1)} async-done(((bf16[64,24,256]{2,1,0:T(8,128)(2,1)}), bf16[256,24,256]{2,1,0:T(8,128)(2,1)}) %all-gather.5.cloned.1.call-update) | async-done | bytes 3145744 | tf_op jit(solution)/shard_map/all_gather | solution.py:528
  88.0 7.7 %project_rows.1 = bf16[64,3,8,896]{3,2,1,0:T(8,128)(2,1)} custom-call(bf16[4,64,3,8,256]{4,3,2,1,0:T(8,128)(2,1)} %bitcast.18, bf16[2,1024,896]{2,1,0:T(8,128)(2,1)} %weights_hbm.1), custom_call_target="tpu_custom_call" | custom-call | flops 4000000000 | bytes 10000000 | tf_op jit(solution)/shard_map/project_rows/pallas_call | solution.py:206
  95.7 0.0 all-to-all-done.3
  95.8 0.0 copy-start.2
  95.8 1.0 copy-done.2
  96.8 10.7 %all-to-all-start.1 = ((bf16[64,24,896]{2,1,0:T(8,128)(2,1)}), bf16[64,24,896]{2,1,0:T(8,128)(2,1)S(1)}, u32[]{:S(2)}, u32[]{:S(2)}) async-start(bf16[64,24,896]{2,1,0:T(8,128)(2,1)} %bitcast.15), calls=%async_computation.1 | async-start | bytes 5505024 | tf_op jit(solution)/shard_map/all_to_all | solution.py:500
  107.5 0.0 all-gather.7.cloned.1.call-start
  107.5 0.7 all-gather.7.cloned.1.call-update
  108.2 0.1 select_reduce_fusion.members_ref
  108.3 64.2 %all-to-all-done.1 = bf16[64,24,896]{2,1,0:T(8,128)(2,1)S(1)} async-done(((bf16[64,24,896]{2,1,0:T(8,128)(2,1)}), bf16[64,24,896]{2,1,0:T(8,128)(2,1)S(1)}, u32[]{:S(2)}, u32[]{:S(2)}) %all-to-all-start.1) | async-done | bytes 2752544 | tf_op jit(solution)/shard_map/all_to_all | solution.py:500
  172.6 2.9 regroup_rows.1.after_ref
  175.5 5.9 %all-to-all-start.2 = ((bf16[64,32,8,128]{3,2,1,0:T(8,128)(2,1)}), bf16[64,32,8,128]{3,2,1,0:T(8,128)(2,1)}, u32[]{:S(2)}, u32[]{:S(2)}) async-start(bf16[64,32,8,128]{3,2,1,0:T(8,128)(2,1)} %regroup_rows.1.after_ref), calls=%async_computation.2 | async-start | bytes 8388608 | tf_op jit(solution)/shard_map/all_to_all | solution.py:500
  181.4 0.0 all-gather.7.cloned.1.call-done
  181.4 69.7 %invert_gram.1.maps_hbm = bf16[2048,2304]{1,0:T(8,128)(2,1)} custom-call(bf16[4,64,5,8,256]{4,3,2,1,0:T(8,128)(2,1)} %bitcast.17, bf16[64,32,8,128]{3,2,1,0:T(8,128)(2,1)} %regroup_rows.1.after_ref), custom_call_target="tpu_custom_call" | custom-call | flops 60000002048 | bytes 16000000 | tf_op jit(solution)/shard_map/invert_gram/pallas_call | solution.py:393
  251.1 26.2 %all-to-all-done.2.packed_hbm = bf16[64,32,8,128]{3,2,1,0:T(8,128)(2,1)} async-done(((bf16[64,32,8,128]{3,2,1,0:T(8,128)(2,1)}), bf16[64,32,8,128]{3,2,1,0:T(8,128)(2,1)}, u32[]{:S(2)}, u32[]{:S(2)}) %all-to-all-start.2) | async-done | bytes 4194336 | tf_op jit(solution)/shard_map/all_to_all | solution.py:500
  277.3 15.9 %merge_rows.1 = bf16[1024,896]{1,0:T(8,128)(2,1)} custom-call(bf16[64,32,8,128]{3,2,1,0:T(8,128)(2,1)} %all-to-all-done.2.packed_hbm, bf16[2048,2304]{1,0:T(8,128)(2,1)} %invert_gram.1.maps_hbm), custom_call_target="tpu_custom_call" | custom-call | flops 9400000512 | bytes 16000000 | tf_op jit(solution)/shard_map/merge_rows/pallas_call | solution.py:462
  (8 shorter events, 0.0 us)
Async XLA Ops:
  7.4 4.4 %copy-start = (s32[1,1024]{1,0:T(1,128)}, s32[1,1024]{1,0:T(1,128)S(1)}, u32[]{:S(2)}) copy-start(s32[1,1024]{1,0:T(1,128)S(1)} %reshape.101.routes_ref) | copy-start | bytes 12292
  7.6 1.0 copy-start.1
  8.6 16.3 %copy-start.4 = (s32[128]{0:T(128)S(1)}, s32[128]{0:T(128)}, u32[]{:S(2)}) copy-start(s32[128]{0:T(128)} %param.7) | copy-start | bytes 1540
  11.8 36.0 %all-to-all-start = ((bf16[64,24,256]{2,1,0:T(8,128)(2,1)}), bf16[64,24,256]{2,1,0:T(8,128)(2,1)S(1)}, u32[]{:S(2)}, u32[]{:S(2)}) async-start(bf16[64,24,256]{2,1,0:T(8,128)(2,1)} %bitcast.1), calls=%async_computation | async-start | bytes 1572864 | tf_op jit(solution)/shard_map/all_to_all | solution.py:500
  24.8 63.2 %all-gather.5.cloned.1.call-start = ((), (), s32[]{:S(2)}) async-start(), calls=%async_computation.4 | async-start | bytes 3932160 | tf_op jit(solution)/shard_map/all_gather | solution.py:528
  47.8 0.9 copy-start.3
  48.7 47.0 %all-to-all-start.3 = ((bf16[64,40,256]{2,1,0:T(8,128)(2,1)}), bf16[64,40,256]{2,1,0:T(8,128)(2,1)S(1)}, u32[]{:S(2)}, u32[]{:S(2)}) async-start(bf16[64,40,256]{2,1,0:T(8,128)(2,1)} %bitcast.16), calls=%async_computation.3 | async-start | bytes 2621440 | tf_op jit(solution)/shard_map/all_to_all | solution.py:500
  95.8 1.1 copy-start.2
  96.8 75.7 %all-to-all-start.1 = ((bf16[64,24,896]{2,1,0:T(8,128)(2,1)}), bf16[64,24,896]{2,1,0:T(8,128)(2,1)S(1)}, u32[]{:S(2)}, u32[]{:S(2)}) async-start(bf16[64,24,896]{2,1,0:T(8,128)(2,1)} %bitcast.15), calls=%async_computation.1 | async-start | bytes 5505024 | tf_op jit(solution)/shard_map/all_to_all | solution.py:500
  107.5 74.0 %all-gather.7.cloned.1.call-start = ((), (), s32[]{:S(2)}) async-start(), calls=%async_computation.5 | async-start | bytes 6553600 | tf_op jit(solution)/shard_map/all_gather | solution.py:535
  175.5 101.8 %all-to-all-start.2 = ((bf16[64,32,8,128]{3,2,1,0:T(8,128)(2,1)}), bf16[64,32,8,128]{3,2,1,0:T(8,128)(2,1)}, u32[]{:S(2)}, u32[]{:S(2)}) async-start(bf16[64,32,8,128]{3,2,1,0:T(8,128)(2,1)} %regroup_rows.1.after_ref), calls=%async_computation.2 | async-start | bytes 8388608 | tf_op jit(solution)/shard_map/all_to_all | solution.py:500
Sparse Core Ops, SparseCore 0:
  48.9 39.1 all-gather.4
  110.1 59.3 all-gather.6
